TPU v7x, 32 devices: a whole 2x2x4 slice. The times are simulated.
32 devices in a mesh: col: 8 (over z, y), row: 4 (over x, core).
Axes of the slice: x: 2, y: 2, z: 4, core: 2. Of those that a mesh axis runs over, the one named last changes fastest.
Arguments:
- hamiltonian: float32 [16384, 16384], P('row', 'col'), as said below
Outputs:
- reduced: float32 [16384, 16384], P('row', 'col')
Inputs may be any that keep to these rules, and one draw needn't show every extreme that they name: hamiltonian is symmetric.
All inputs are finite; a program needn't handle non-finite values.
Results may differ from a plain program's by a relative error of at most 0.00019.
Values sent between devices are 32-bit elements; how exact they have to be, the bound alone decides.
A program may use at most 192 MiB of HBM per device.

v0:
```python
import jax
import jax.numpy as jnp
from jax import lax
from jax.sharding import PartitionSpec as P

NB = 256
PANELS = 2


def from_root(block, axis, holder):
    block = jnp.where(lax.axis_index(axis) == holder, block, jnp.zeros_like(block))
    return lax.psum(block, axis)


def product(left, right):
    return jnp.dot(left, right, precision=lax.Precision.HIGHEST, preferred_element_type=jnp.float32)


def inner_tn(left, right):
    return lax.dot_general(
        left,
        right,
        (((0,), (0,)), ((), ())),
        precision=lax.Precision.HIGHEST,
        preferred_element_type=jnp.float32,
    )


def outer_nt(left, right):
    return lax.dot_general(
        left,
        right,
        (((1,), (1,)), ((), ())),
        precision=lax.Precision.HIGHEST,
        preferred_element_type=jnp.float32,
    )


def solve_right(gram, panel):
    lower = jnp.linalg.cholesky(gram)
    return lax.linalg.triangular_solve(lower, panel, left_side=False, lower=True, transpose_a=True)


def coupling_of(top_rows):
    square = jnp.eye(NB, dtype=jnp.float32) - top_rows.T
    normal_eq = inner_tn(square, square)
    factor = jnp.linalg.cholesky(normal_eq)
    middle = lax.linalg.triangular_solve(factor, square.T, left_side=True, lower=True)
    return lax.linalg.triangular_solve(factor, middle, left_side=True, lower=True, transpose_a=True)


def shards(hamiltonian):
    matrix = hamiltonian
    row_block = matrix.shape[0]
    col_block = matrix.shape[1]
    ratio = lax.axis_size("col") // lax.axis_size("row")
    row_pos = lax.axis_index("row")
    col_pos = lax.axis_index("col")
    global_rows = row_pos * row_block + jnp.arange(row_block, dtype=jnp.int32)
    owner = col_pos // ratio
    offset = col_pos % ratio * col_block
    for panel_index in range(PANELS):
        first_col = panel_index * NB
        first_row = first_col + NB
        live = (global_rows >= first_row)[:, None]
        panel = jnp.where(live, matrix[:, first_col : first_col + NB], jnp.float32(0.0))
        gram = lax.psum(inner_tn(panel, panel), "row")
        basis = solve_right(gram, panel)
        top_rows = from_root(basis[first_row : first_row + NB], "row", 0)
        coupling = coupling_of(top_rows)
        ident = (
            global_rows[:, None] - first_row == jnp.arange(NB, dtype=jnp.int32)[None, :]
        ).astype(jnp.float32)
        vectors = ident - basis
        vectors, coupling = (from_root(vectors, "col", 0), from_root(coupling, "col", 0))
        column_vectors = from_root(
            lax.dynamic_slice_in_dim(vectors, offset, col_block, 0), "row", owner
        )
        applied = lax.psum(product(matrix, column_vectors), "col")
        applied = product(applied, coupling)
        inner = lax.psum(inner_tn(vectors, applied), "row")
        inner = product(coupling.T, inner)
        shifted = applied - 0.5 * product(vectors, inner)
        column_shifted = from_root(
            lax.dynamic_slice_in_dim(shifted, offset, col_block, 0), "row", owner
        )
        matrix = matrix - outer_nt(vectors, column_shifted) - outer_nt(shifted, column_vectors)
    return matrix


def solution(mesh):
    return jax.shard_map(
        shards,
        mesh=mesh,
        in_specs=(P("row", "col"),),
        out_specs=P("row", "col"),
        check_vma=False,
    )
```

profile of v0, /device:TPU:2, one launch (start us, length us, event | category | flops | bytes accessed | tf_op | source)
XLA Modules:
  0.0 1654.2 jit_solution(16838280253457113828)
XLA Ops:
  6.5 31.1 %copy.10 = f32[4096,2048]{0,1:T(8,128)} copy(f32[4096,2048]{1,0:T(8,128)} %param.8) | data formatting | bytes 67108864 | tf_op args[0]
  42.1 4.2 fusion.60
  46.6 31.7 %all-reduce.18.cloned.1.call-done = f32[256,256]{0,1:T(8,128)} async-done(((f32[256,256]{0,1:T(8,128)}), f32[256,256]{0,1:T(8,128)}) %all-reduce.18.cloned.1.call-update) | async-done | bytes 262160 | tf_op jit(solution)/shard_map/psum | solution.py:67
  80.3 11.7 cholesky.214
  92.1 9.8 custom-call.23
  102.4 11.7 cholesky.231
  116.2 4.1 while.12
  120.3 19.7 %custom-call.24 = f32[2,128,128]{1,2,0:T(8,128)S(1)} custom-call(f32[2,128,128]{2,1,0:T(8,128)S(1)} %get-tuple-element.51), custom_call_target="InvertDiagBlocksLowerTriangular" | custom-call | tf_op jit(solution)/shard_map/triangular_solve/custom-call.0 | solution.py:41
  153.2 156.2 %all-reduce.20.cloned.1.call-done = f32[4096,256]{0,1:T(8,128)} async-done(((f32[4096,256]{0,1:T(8,128)}), f32[4096,256]{0,1:T(8,128)}) %all-reduce.20.cloned.1.call-update) | async-done | bytes 4194320 | tf_op jit(solution)/shard_map/psum | solution.py:12
  313.0 53.5 %all-reduce.40.cloned.1.call-done = (f32[2048,256]{0,1:T(8,128)}, f32[256,256]{0,1:T(8,128)}) async-done(((f32[2048,256]{0,1:T(8,128)}, f32[256,256]{0,1:T(8,128)}), (f32[2048,256]{0,1:T(8,128)}, f32[256,256]{0,1:T(8,128)})) %all-reduce.40.cloned.1.call-update) | async-done | bytes 2359312 | tf_op jit(solution)/shard_map/psum | solution.py:12
  369.4 11.7 cholesky.248
  381.2 9.8 custom-call.25
  391.5 11.7 cholesky.265
  409.9 19.7 %custom-call.27 = f32[2,128,128]{1,2,0:T(8,128)S(1)} custom-call(f32[2,128,128]{2,1,0:T(8,128)S(1)} %get-tuple-element.53), custom_call_target="InvertDiagBlocksLowerTriangular" | custom-call | tf_op jit(solution)/shard_map/triangular_solve/custom-call.5 | solution.py:49
  431.7 33.2 %convolution_bitcast_fusion = f32[4096,256]{0,1:T(8,128)} fusion(f32[2048,256]{0,1:T(8,128)S(1)} %copy-done.13, f32[4096,2048]{1,0:T(8,128)} %param.8), kind=kOutput, calls=%fused_computation.14 | convolution fusion | flops 25769803776 | bytes 39845888 | tf_op jit(solution)/shard_map/dot_general | solution.py:16
  465.7 164.8 %all-reduce.36.cloned.1.call-done = (f32[4096,256]{0,1:T(8,128)}, f32[256,256]{0,1:T(8,128)}) async-done(((f32[4096,256]{0,1:T(8,128)}, f32[256,256]{0,1:T(8,128)}), (f32[4096,256]{0,1:T(8,128)}, f32[256,256]{0,1:T(8,128)})) %all-reduce.36.cloned.1.call-update) | async-done | bytes 4456464 | tf_op jit(solution)/shard_map/psum | solution.py:79
  630.5 8.8 fusion.61
  641.3 4.3 fusion.62
  645.7 5.6 copy.9
  651.4 24.0 %all-reduce.22.cloned.1.call-done = f32[256,256]{1,0:T(8,128)} async-done(((f32[256,256]{1,0:T(8,128)}), f32[256,256]{1,0:T(8,128)}) %all-reduce.22.cloned.1.call-update) | async-done | bytes 262160 | tf_op jit(solution)/shard_map/psum | solution.py:81
  676.7 8.0 fusion.1
  688.3 51.8 %all-reduce.24.cloned.1.call-done = f32[2048,256]{0,1:T(8,128)} async-done(((f32[2048,256]{0,1:T(8,128)}), f32[2048,256]{0,1:T(8,128)}) %all-reduce.24.cloned.1.call-update) | async-done | bytes 2097168 | tf_op jit(solution)/shard_map/psum | solution.py:12
  740.1 32.8 %fusion.64 = f32[4096,2048]{0,1:T(8,128)} fusion(f32[4096,256]{0,1:T(8,128)} %all-reduce.20.cloned.1.call-done, f32[2048,256]{0,1:T(8,128)} %all-reduce.24.cloned.1.call-done), kind=kOutput, calls=%fused_computation.158 | convolution fusion | flops 25769803776 | bytes 39845888 | tf_op jit(solution)/shard_map/dot_general | solution.py:30
  772.9 42.5 %subtract_subtract_fusion.1 = f32[4096,2048]{0,1:T(8,128)} fusion(f32[4096,2048]{0,1:T(8,128)} %copy.10, f32[4096,2048]{0,1:T(8,128)} %fusion.64, f32[4096,256]{0,1:T(8,128)} %copy-done.8, f32[2048,256]{0,1:T(8,128)S(1)} %copy-done.13), kind=kOutput, calls=%fused_computation.9 | convolution fusion | flops 25786580992 | bytes 106954752 | tf_op jit(solution)/shard_map/dot_general | solution.py:30
  819.9 4.2 fusion.65
  824.4 31.6 %all-reduce.26.cloned.1.call-done = f32[256,256]{0,1:T(8,128)} async-done(((f32[256,256]{0,1:T(8,128)}), f32[256,256]{0,1:T(8,128)}) %all-reduce.26.cloned.1.call-update) | async-done | bytes 262160 | tf_op jit(solution)/shard_map/psum | solution.py:67
  858.0 11.7 cholesky.282
  869.8 9.8 custom-call.28
  880.1 11.7 cholesky.299
  894.5 4.3 while.14
  898.7 19.7 %custom-call.29 = f32[2,128,128]{1,2,0:T(8,128)S(1)} custom-call(f32[2,128,128]{2,1,0:T(8,128)S(1)} %get-tuple-element.54), custom_call_target="InvertDiagBlocksLowerTriangular" | custom-call | tf_op jit(solution)/shard_map/triangular_solve/custom-call.0 | solution.py:41
  931.6 156.2 %all-reduce.28.cloned.1.call-done = f32[4096,256]{0,1:T(8,128)} async-done(((f32[4096,256]{0,1:T(8,128)}), f32[4096,256]{0,1:T(8,128)}) %all-reduce.28.cloned.1.call-update) | async-done | bytes 4194320 | tf_op jit(solution)/shard_map/psum | solution.py:12
  1091.2 53.7 %all-reduce.38.cloned.1.call-done = (f32[2048,256]{0,1:T(8,128)}, f32[256,256]{0,1:T(8,128)}) async-done(((f32[2048,256]{0,1:T(8,128)}, f32[256,256]{0,1:T(8,128)}), (f32[2048,256]{0,1:T(8,128)}, f32[256,256]{0,1:T(8,128)})) %all-reduce.38.cloned.1.call-update) | async-done | bytes 2359312 | tf_op jit(solution)/shard_map/psum | solution.py:12
  1147.9 11.7 cholesky.316
  1159.6 9.8 custom-call.30
  1169.9 11.7 cholesky.333
  1188.0 19.7 %custom-call.32 = f32[2,128,128]{1,2,0:T(8,128)S(1)} custom-call(f32[2,128,128]{2,1,0:T(8,128)S(1)} %get-tuple-element.56), custom_call_target="InvertDiagBlocksLowerTriangular" | custom-call | tf_op jit(solution)/shard_map/triangular_solve/custom-call.5 | solution.py:49
  1209.8 57.5 %fusion.66 = f32[4096,256]{1,0:T(8,128)} fusion(f32[4096,2048]{0,1:T(8,128)} %subtract_subtract_fusion.1, f32[2048,256]{0,1:T(8,128)S(1)} %copy-done.12), kind=kOutput, calls=%fused_computation.160 | convolution fusion | flops 25769803776 | bytes 39845888 | tf_op jit(solution)/shard_map/dot_general | solution.py:16
  1268.1 164.7 %all-reduce.34.cloned.1.call-done = (f32[4096,256]{1,0:T(8,128)}, f32[256,256]{0,1:T(8,128)}) async-done(((f32[4096,256]{1,0:T(8,128)}, f32[256,256]{0,1:T(8,128)}), (f32[4096,256]{1,0:T(8,128)}, f32[256,256]{0,1:T(8,128)})) %all-reduce.34.cloned.1.call-update) | async-done | bytes 4456464 | tf_op jit(solution)/shard_map/psum | solution.py:79
  1432.8 5.4 fusion.67
  1440.3 4.3 fusion.68
  1444.7 5.6 copy.19
  1450.3 24.0 %all-reduce.30.cloned.1.call-done = f32[256,256]{1,0:T(8,128)} async-done(((f32[256,256]{1,0:T(8,128)}), f32[256,256]{1,0:T(8,128)}) %all-reduce.30.cloned.1.call-update) | async-done | bytes 262160 | tf_op jit(solution)/shard_map/psum | solution.py:81
  1475.7 8.0 fusion
  1487.2 51.9 %all-reduce.32.cloned.1.call-done = f32[2048,256]{0,1:T(8,128)} async-done(((f32[2048,256]{0,1:T(8,128)}), f32[2048,256]{0,1:T(8,128)}) %all-reduce.32.cloned.1.call-update) | async-done | bytes 2097168 | tf_op jit(solution)/shard_map/psum | solution.py:12
  1539.0 32.4 %fusion.70 = f32[4096,2048]{0,1:T(8,128)} fusion(f32[4096,256]{0,1:T(8,128)} %all-reduce.28.cloned.1.call-done, f32[2048,256]{0,1:T(8,128)} %all-reduce.32.cloned.1.call-done), kind=kOutput, calls=%fused_computation.164 | convolution fusion | flops 25769803776 | bytes 39845888 | tf_op jit(solution)/shard_map/dot_general | solution.py:30
  1571.4 42.4 %subtract_subtract_fusion = f32[4096,2048]{0,1:T(8,128)} fusion(f32[4096,2048]{0,1:T(8,128)} %subtract_subtract_fusion.1, f32[4096,2048]{0,1:T(8,128)} %fusion.70, f32[4096,256]{0,1:T(8,128)} %copy-done.9, f32[2048,256]{0,1:T(8,128)S(1)} %copy-done.12), kind=kOutput, calls=%fused_computation.8 | convolution fusion | flops 25786580992 | bytes 106954752 | tf_op jit(solution)/shard_map/dot_general | solution.py:30
  1613.8 33.3 %copy.22 = f32[4096,2048]{1,0:T(8,128)} copy(f32[4096,2048]{0,1:T(8,128)} %subtract_subtract_fusion) | data formatting | bytes 67108864 | tf_op jit(solution)/shard_map/sub | solution.py:87
  (173 shorter events, 102.0 us)
Async XLA Ops:
  6.5 71.7 %all-reduce.18.cloned.1.call-start = ((), (), s32[]{:S(2)}) async-start(), calls=%async_computation | async-start | bytes 524288 | tf_op jit(solution)/shard_map/psum | solution.py:67
  40.1 1.9 copy-start
  46.3 263.1 %all-reduce.20.cloned.1.call-start = ((), (), s32[]{:S(2)}) async-start(), calls=%async_computation.1 | async-start | bytes 8388608 | tf_op jit(solution)/shard_map/psum | solution.py:12
  140.0 3.7 copy-start.1
  147.6 1.3 copy-start.10
  151.5 215.0 %all-reduce.40.cloned.1.call-start = ((), (), s32[]{:S(2)}) async-start(), calls=%async_computation.11 | async-start | bytes 4718592 | tf_op jit(solution)/shard_map/psum | solution.py:12
  312.5 318.0 %all-reduce.36.cloned.1.call-start = ((), (), s32[]{:S(2)}) async-start(), calls=%async_computation.9 | async-start | bytes 8912896 | tf_op jit(solution)/shard_map/psum | solution.py:79
  366.4 65.2 %copy-start.13 = (f32[2048,256]{0,1:T(8,128)S(1)}, f32[2048,256]{0,1:T(8,128)}, u32[]{:S(2)}) copy-start(f32[2048,256]{0,1:T(8,128)} %get-tuple-element.95) | copy-start | bytes 6291460
  465.7 209.7 %all-reduce.22.cloned.1.call-start = ((), (), s32[]{:S(2)}) async-start(), calls=%async_computation.2 | async-start | bytes 524288 | tf_op jit(solution)/shard_map/psum | solution.py:81
  630.5 10.8 copy-start.4
  639.3 2.0 copy-start.6
  645.7 29.7 %copy-start.14 = (f32[256,256]{0,1:T(8,128)S(1)}, f32[256,256]{0,1:T(8,128)}, u32[]{:S(2)}) copy-start(f32[256,256]{0,1:T(8,128)} %get-tuple-element.92) | copy-start | bytes 786436
  645.7 94.4 %all-reduce.24.cloned.1.call-start = ((), (), s32[]{:S(2)}) async-start(), calls=%async_computation.3 | async-start | bytes 4194304 | tf_op jit(solution)/shard_map/psum | solution.py:12
  684.8 1.9 copy-start.8
  688.2 167.7 %all-reduce.26.cloned.1.call-start = ((), (), s32[]{:S(2)}) async-start(), calls=%async_computation.4 | async-start | bytes 524288 | tf_op jit(solution)/shard_map/psum | solution.py:67
  817.9 1.9 copy-start.2
  824.1 263.7 %all-reduce.28.cloned.1.call-start = ((), (), s32[]{:S(2)}) async-start(), calls=%async_computation.5 | async-start | bytes 8388608 | tf_op jit(solution)/shard_map/psum | solution.py:12
  918.4 3.7 copy-start.3
  926.1 1.3 copy-start.11
  929.9 215.0 %all-reduce.38.cloned.1.call-start = ((), (), s32[]{:S(2)}) async-start(), calls=%async_computation.10 | async-start | bytes 4718592 | tf_op jit(solution)/shard_map/psum | solution.py:12
  1091.0 341.9 %all-reduce.34.cloned.1.call-start = ((), (), s32[]{:S(2)}) async-start(), calls=%async_computation.8 | async-start | bytes 8912896 | tf_op jit(solution)/shard_map/psum | solution.py:79
  1144.9 64.9 %copy-start.12 = (f32[2048,256]{0,1:T(8,128)S(1)}, f32[2048,256]{0,1:T(8,128)}, u32[]{:S(2)}) copy-start(f32[2048,256]{0,1:T(8,128)} %get-tuple-element.93) | copy-start | bytes 6291460
  1268.1 206.3 %all-reduce.30.cloned.1.call-start = ((), (), s32[]{:S(2)}) async-start(), calls=%async_computation.6 | async-start | bytes 524288 | tf_op jit(solution)/shard_map/psum | solution.py:81
  1432.8 7.4 copy-start.5
  1438.3 2.0 copy-start.7
  1444.6 29.7 %copy-start.15 = (f32[256,256]{0,1:T(8,128)S(1)}, f32[256,256]{0,1:T(8,128)}, u32[]{:S(2)}) copy-start(f32[256,256]{0,1:T(8,128)} %get-tuple-element.90) | copy-start | bytes 786436
  1444.6 94.4 %all-reduce.32.cloned.1.call-start = ((), (), s32[]{:S(2)}) async-start(), calls=%async_computation.7 | async-start | bytes 4194304 | tf_op jit(solution)/shard_map/psum | solution.py:12
  1483.7 1.9 copy-start.9
Sparse Core Ops, SparseCore 0:
  46.4 31.7 all-reduce.17
  151.6 157.7 all-reduce.19
  312.6 53.7 all-reduce.39
  465.8 164.6 all-reduce.35
  645.8 29.5 all-reduce.21
  688.3 51.7 all-reduce.23
  824.2 31.6 all-reduce.25
  930.1 157.7 all-reduce.27
  1091.1 53.7 all-reduce.37
  1268.2 164.6 all-reduce.33
  1444.7 29.5 all-reduce.29
  1487.3 51.7 all-reduce.31
where the time goes:
time: 1660 us; the launch traced here: 1650 us
  waiting for transfers between devices  964 us (58%)
  matrix products  316 us (19%)
  other arithmetic  244 us (15%)
  local copies, waits for them, and re-layouts  108 us (7%)
  between operations  19.4 us (1%)
    psum x6, waiting for transfers between devices, from_root(): return lax.psum(block, axis)  523 us
    psum x2, waiting for transfers between devices, shards(): applied = lax.psum(product(matrix, column_vectors), 'col')  329 us
    dot_general x4, matrix products, outer_nt(): lax.dot_general(left, right, (((1,), (1,)), ((), ())), precision=lax.Prec...  150 us
    dot_general x8, matrix products, product(): jnp.dot(left, right, precision=lax.Precision.HIGHEST, preferred_element_t...  124 us
    another operation x14, other arithmetic, coupling_of(): factor = jnp.linalg.cholesky(normal_eq)  69.2 us
    another operation x13, other arithmetic, solve_right(): lower = jnp.linalg.cholesky(gram)  68.6 us
    psum x2, waiting for transfers between devices, shards(): gram = lax.psum(inner_tn(panel, panel), 'row')  63.2 us
    psum x2, waiting for transfers between devices, shards(): inner = lax.psum(inner_tn(vectors, applied), 'row')  48 us
  transfers between devices with their start and end apart: 12, of which 12 were waited for; matrix products, arithmetic and copies ran while one was open for 1% of the time, Pallas kernels for 0%

commit v1 on v0

v1 whole, which is shorter than its diff:
```python
import jax
import jax.numpy as jnp
from jax import lax
from jax.sharding import PartitionSpec as P

NB = 256
PANELS = 2
CHUNKS = 2
BOTH = ("col", "row")


def mm(left, right, dims, precision=lax.Precision.HIGHEST):
    return lax.dot_general(
        left,
        right,
        ((dims[0], dims[1]), ((), ())),
        precision=precision,
        preferred_element_type=jnp.float32,
    )


def nn(left, right, precision=lax.Precision.HIGHEST):
    return mm(left, right, ((1,), (0,)), precision)


def nt(left, right, precision=lax.Precision.HIGHEST):
    return mm(left, right, ((1,), (1,)), precision)


def tn(left, right, precision=lax.Precision.HIGHEST):
    return mm(left, right, ((0,), (0,)), precision)


def inverse_factor(gram):
    lower = jnp.linalg.cholesky(gram)
    eye = jnp.eye(NB, dtype=jnp.float32)
    return lax.linalg.triangular_solve(lower, eye, left_side=True, lower=True)


def small_factors(gram, top):
    inv = inverse_factor(gram)
    basis_top = nt(top, inv)
    square = jnp.eye(NB, dtype=jnp.float32) - basis_top.T
    inv2 = inverse_factor(tn(square, square))
    coupling = tn(inv2, nt(inv2, square))
    return inv, basis_top, coupling


def to_rows(block, rows, ratio):
    swap = [
        ((ratio * i + q) * rows + s, (ratio * s + q) * rows + i)
        for s in range(rows)
        for i in range(rows)
        for q in range(ratio)
    ]
    place = lax.axis_index("col") % ratio
    height = block.shape[0] // CHUNKS
    out = []
    for chunk in range(CHUNKS):
        own = lax.ppermute(block[chunk * height : (chunk + 1) * height], BOTH, swap)
        parts = [own]
        for step in range(1, ratio):
            turn = [
                (ratio * s + q, ratio * s + (q + step) % ratio)
                for s in range(rows)
                for q in range(ratio)
            ]
            parts.append(lax.ppermute(own, "col", turn))
        ordered = []
        for q in range(ratio):
            piece = parts[0]
            for step in range(1, ratio):
                piece = jnp.where((place - q) % ratio == step, parts[step], piece)
            ordered.append(piece)
        out.append(jnp.concatenate(ordered, axis=1))
    return jnp.concatenate(out, axis=0)


def unit_rows(ids, first_row):
    return (jnp.arange(NB, dtype=jnp.int32)[:, None] + first_row == ids[None, :]).astype(jnp.float32)


def shards(matrix):
    row_block, col_block = matrix.shape
    rows = lax.axis_size("row")
    ratio = lax.axis_size("col") // rows
    row_pos = lax.axis_index("row")
    col_pos = lax.axis_index("col")
    row_ids = row_pos * row_block + jnp.arange(row_block, dtype=jnp.int32)
    col_ids = col_pos * col_block + jnp.arange(col_block, dtype=jnp.int32)
    high = lax.Precision.HIGH

    def from_first_row(block):
        return lax.psum(jnp.where(row_pos == 0, block, 0.0), "row")

    def columns_of(block, first):
        start = first % col_block
        return jnp.where(col_pos == first // col_block, block[:, start : start + NB], 0.0)

    first_c = from_first_row(matrix[:NB])
    panel = jnp.where((row_ids >= NB)[:, None], matrix[:, :NB], 0.0)
    top = jnp.where(row_pos == 0, matrix[NB : 2 * NB, :NB], 0.0)
    sums = lax.psum(jnp.where(col_pos == 0, jnp.concatenate([tn(panel, panel), top]), 0.0), BOTH)
    first_r = to_rows(first_c, rows, ratio)
    second_c = from_first_row(lax.optimization_barrier((matrix[NB : 2 * NB], first_c))[0])
    second_r = to_rows(lax.optimization_barrier((second_c, first_r))[0], rows, ratio)

    inv, basis_top, coupling = small_factors(sums[:NB], sums[NB:])
    v1_r = unit_rows(row_ids, NB) - nn(inv, jnp.where(row_ids >= NB, first_r, 0.0))
    v1_c = unit_rows(col_ids, NB) - nn(inv, jnp.where(col_ids >= NB, first_c, 0.0))
    partial = nn(v1_r, matrix, high)
    z_c = lax.psum(partial, "row")
    z_top = columns_of(partial, NB)
    sums = lax.psum(jnp.concatenate([nt(v1_c, partial), z_top]), BOTH)
    v1_top = jnp.eye(NB, dtype=jnp.float32) - basis_top
    inner = nn(tn(coupling, sums[:NB]), coupling)
    s1_top = tn(sums[NB:], coupling) - 0.5 * nn(v1_top, inner)
    s1_c = tn(coupling, z_c) - 0.5 * tn(inner, v1_c)

    p2_c = second_c - nn(s1_top, v1_c) - nn(v1_top, s1_c)
    p2_c = jnp.where(col_ids >= 2 * NB, p2_c, 0.0)
    top = columns_of(p2_c, 2 * NB).T
    sums = lax.psum(jnp.concatenate([nt(p2_c, p2_c), top]), "col")
    s1_r = to_rows(s1_c, rows, ratio)
    p2_r = second_r - nn(s1_top, v1_r) - nn(v1_top, s1_r)
    p2_r = jnp.where(row_ids >= 2 * NB, p2_r, 0.0)

    inv, basis_top, coupling = small_factors(sums[:NB], sums[NB:])
    v2_r = unit_rows(row_ids, 2 * NB) - nn(inv, p2_r)
    v2_c = unit_rows(col_ids, 2 * NB) - nn(inv, p2_c)
    partial = nn(v2_r, matrix, high) - nn(nt(v2_r, s1_r), v1_c) - nn(nt(v2_r, v1_r), s1_c)
    z_c = lax.psum(partial, "row")
    inner = lax.psum(nt(v2_c, partial), BOTH)
    inner = nn(tn(coupling, inner), coupling)
    s2_c = tn(coupling, z_c) - 0.5 * tn(inner, v2_c)
    s2_r = to_rows(s2_c, rows, ratio)

    early = tn(
        jnp.concatenate([v1_r, s1_r, v2_r]), jnp.concatenate([s1_c, v1_c, s2_c]), high
    )
    return (matrix - early) - tn(s2_r, v2_c, high)


def solution(mesh):
    return jax.shard_map(
        shards,
        mesh=mesh,
        in_specs=(P("row", "col"),),
        out_specs=P("row", "col"),
        check_vma=False,
    )
```

time: 1660 us -> 1440 us (0.87)
  waiting for transfers between devices: 964 us -> 841 us
  local copies, waits for them, and re-layouts: 108 us -> 31.9 us
  matrix products: 316 us -> 240 us
  starting transfers between devices: 1.43 us -> 40.8 us
    psum x12 -> x7, waiting for transfers between devices: 964 us -> 644 us  [the longest x1 144 us: shards(): sums = lax.psum(jnp.concatenate([nt(p2_c, p2_c), top]), 'col')]
    ppermute x0 -> x16, waiting for transfers between devices: none -> 197 us  [the longest x8 138 us: to_rows(): own = lax.ppermute(block[chunk * height:(chunk + 1) * height], BOTH, swap)]
    dot_general x18 -> x38, matrix products: 294 us -> 232 us  [mm(): lax.dot_general(left, right, ((dims[0], dims[1]), ((), ())), precision=pr...]
    unnamed x33 -> x60, local copies, waits for them, and re-layouts: 45.4 us -> 2.13 us
    ppermute x0 -> x16, starting transfers between devices: none -> 40.3 us  [the longest x8 31 us: to_rows(): own = lax.ppermute(block[chunk * height:(chunk + 1) * height], BOTH, swap)]
    sub x1 -> x0, local copies, waits for them, and re-layouts: 33.3 us -> none  [shards(): matrix - outer_nt(vectors, column_shifted)]
  transfers between devices with their start and end apart: 12 -> 23, of which waited for: 12 -> 13; matrix products, arithmetic and copies ran while one was open for 1% -> 25% of each run, Pallas kernels for 0% -> 0%
where the time goes in v1:
time: 1440 us; the launch traced here: 1430 us
  waiting for transfers between devices  841 us (58%)
  other arithmetic  251 us (17%)
  matrix products  240 us (17%)
  starting transfers between devices  40.8 us (3%)
  local copies, waits for them, and re-layouts  31.9 us (2%)
  between operations  20.1 us (1%)
    dot_general x38, matrix products, mm(): lax.dot_general(left, right, ((dims[0], dims[1]), ((), ())), precision=pr...  232 us
    psum x1, waiting for transfers between devices, shards(): sums = lax.psum(jnp.concatenate([nt(p2_c, p2_c), top]), 'col')  144 us
    another operation x27, other arithmetic, inverse_factor(): lower = jnp.linalg.cholesky(gram)  139 us
    ppermute x8, waiting for transfers between devices, to_rows(): own = lax.ppermute(block[chunk * height:(chunk + 1) * height], BOTH, swap)  138 us
    psum x1, waiting for transfers between devices, shards(): sums = lax.psum(jnp.concatenate([nt(v1_c, partial), z_top]), BOTH)  131 us
    psum x2, waiting for transfers between devices, shards(): z_c = lax.psum(partial, 'row')  123 us
    psum x1, waiting for transfers between devices, shards(): inner = lax.psum(nt(v2_c, partial), BOTH)  123 us
    psum x1, waiting for transfers between devices, shards(): lax.psum(jnp.where(col_pos == 0, jnp.concatenate([tn(panel, panel), top])...  122 us
  transfers between devices with their start and end apart: 23, of which 13 were waited for; matrix products, arithmetic and copies ran while one was open for 25% of the time, Pallas kernels for 0%

profile of v1, /device:TPU:2, one launch (start us, length us, event | category | flops | bytes accessed | tf_op | source)
XLA Modules:
  0.0 1426.7 jit_solution(13449092535908764271)
XLA Ops:
  7.5 11.3 fusion.34
  19.8 4.8 fusion.124
  27.3 121.7 %all-reduce.10.cloned.1.call-done = f32[512,256]{1,0:T(8,128)} async-done(((f32[512,256]{1,0:T(8,128)}), f32[512,256]{1,0:T(8,128)}) %all-reduce.10.cloned.1.call-update) | async-done | bytes 524304 | tf_op jit(solution)/shard_map/psum | solution.py:103
  151.2 11.7 cholesky.214
  163.0 9.8 custom-call.17
  173.5 11.7 cholesky.231
  187.3 4.5 while.8
  191.9 19.7 %custom-call.18 = f32[2,128,128]{1,2,0:T(8,128)S(1)} custom-call(f32[2,128,128]{2,1,0:T(8,128)S(1)} %get-tuple-element.37), custom_call_target="InvertDiagBlocksLowerTriangular" | custom-call | tf_op jit(solution)/shard_map/triangular_solve/custom-call.0 | solution.py:37
  213.8 11.7 cholesky.248
  225.6 9.8 custom-call.19
  242.0 11.7 cholesky.265
  256.5 4.5 collective-permute-start
  261.0 49.9 %collective-permute-done.2 = f32[128,2048]{1,0:T(8,128)} collective-permute-done((f32[128,2048]{1,0:T(8,128)}, f32[128,2048]{1,0:T(8,128)}, u32[]{:S(2)}, u32[]{:S(2)}) %collective-permute-start.2) | collective-permute-done | bytes 1048608 | tf_op jit(solution)/shard_map/ppermute | solution.py:60
  316.2 19.7 %custom-call.20 = f32[2,128,128]{1,2,0:T(8,128)S(1)} custom-call(f32[2,128,128]{2,1,0:T(8,128)S(1)} %get-tuple-element.38), custom_call_target="InvertDiagBlocksLowerTriangular" | custom-call | tf_op jit(solution)/shard_map/triangular_solve/custom-call.0 | solution.py:37
  342.7 8.6 collective-permute-done.1
  352.7 7.4 convolution_subtract_fusion.1
  360.2 21.1 %fusion.129 = f32[256,2048]{1,0:T(8,128)} fusion(f32[256,4096]{1,0:T(8,128)} %convolution_subtract_fusion.1, f32[4096,2048]{1,0:T(8,128)} %param.4), kind=kOutput, calls=%fused_computation.243 | convolution fusion | flops 12884901888 | bytes 39845888 | tf_op jit(solution)/shard_map/dot_general | solution.py:13
  389.6 131.2 %all-reduce.14.cloned.1.call-done = f32[512,256]{1,0:T(8,128)} async-done(((f32[512,256]{1,0:T(8,128)}), f32[512,256]{1,0:T(8,128)}) %all-reduce.14.cloned.1.call-update) | async-done | bytes 524304 | tf_op jit(solution)/shard_map/psum | solution.py:114
  524.7 8.2 fusion.134
  532.8 74.1 %all-reduce.22.cloned.1.call-done = (f32[256,2048]{1,0:T(8,128)}, f32[256,2048]{1,0:T(8,128)}) async-done(((f32[256,2048]{1,0:T(8,128)}, f32[256,2048]{1,0:T(8,128)}), (f32[256,2048]{1,0:T(8,128)}, f32[256,2048]{1,0:T(8,128)})) %all-reduce.22.cloned.1.call-update) | async-done | bytes 4194320 | tf_op jit(solution)/shard_map/psum | solution.py:112
  621.6 5.3 collective-permute-start.6
  633.4 5.3 collective-permute-start.10
  641.1 144.5 %all-reduce.16.cloned.1.call-done = f32[512,256]{0,1:T(8,128)} async-done(((f32[512,256]{0,1:T(8,128)}), f32[512,256]{0,1:T(8,128)}) %all-reduce.16.cloned.1.call-update) | async-done | bytes 524304 | tf_op jit(solution)/shard_map/psum | solution.py:123
  787.7 11.7 cholesky.282
  799.4 9.8 custom-call.21
  809.7 11.7 cholesky.299
  824.2 5.2 while.10
  829.4 20.1 %custom-call.22 = f32[2,128,128]{1,2,0:T(8,128)S(1)} custom-call(f32[2,128,128]{2,1,0:T(8,128)S(1)} %get-tuple-element.39), custom_call_target="InvertDiagBlocksLowerTriangular" | custom-call | tf_op jit(solution)/shard_map/triangular_solve/custom-call.0 | solution.py:37
  854.8 11.7 cholesky.316
  867.2 9.8 custom-call.23
  879.1 11.7 cholesky.333
  896.3 5.6 while.11
  901.9 20.3 %custom-call.24 = f32[2,128,128]{1,2,0:T(8,128)} custom-call(f32[2,128,128]{2,1,0:T(8,128)S(1)} %get-tuple-element.40), custom_call_target="InvertDiagBlocksLowerTriangular" | custom-call | tf_op jit(solution)/shard_map/triangular_solve/custom-call.0 | solution.py:37
  924.4 4.9 convolution_subtract_fusion.2
  933.1 15.4 %collective-permute-done.5 = f32[128,2048]{1,0:T(8,128)S(1)} collective-permute-done((f32[128,2048]{1,0:T(8,128)}, f32[128,2048]{1,0:T(8,128)S(1)}, u32[]{:S(2)}, u32[]{:S(2)}) %collective-permute-start.5) | collective-permute-done | bytes 1048608 | tf_op jit(solution)/shard_map/ppermute | solution.py:68
  954.1 16.9 %collective-permute-done.11 = f32[128,2048]{1,0:T(8,128)S(1)} collective-permute-done((f32[128,2048]{1,0:T(8,128)}, f32[128,2048]{1,0:T(8,128)S(1)}, u32[]{:S(2)}, u32[]{:S(2)}) %collective-permute-start.11) | collective-permute-done | bytes 1048608 | tf_op jit(solution)/shard_map/ppermute | solution.py:68
  972.4 18.3 %collective-permute-done.9 = f32[128,2048]{1,0:T(8,128)S(1)} collective-permute-done((f32[128,2048]{1,0:T(8,128)}, f32[128,2048]{1,0:T(8,128)S(1)}, u32[]{:S(2)}, u32[]{:S(2)}) %collective-permute-start.9) | collective-permute-done | bytes 1048608 | tf_op jit(solution)/shard_map/ppermute | solution.py:68
  992.1 7.8 convolution_subtract_fusion
  999.9 20.8 %fusion.136 = f32[256,2048]{1,0:T(8,128)} fusion(f32[256,4096]{1,0:T(8,128)} %convolution_subtract_fusion, f32[4096,2048]{1,0:T(8,128)} %param.4), kind=kOutput, calls=%fused_computation.250 | convolution fusion | flops 12884901888 | bytes 39845888 | tf_op jit(solution)/shard_map/dot_general | solution.py:13
  1020.8 7.1 fusion.40
  1036.8 5.3 fusion.139
  1044.2 123.2 %all-reduce.20.cloned.1.call-done = f32[256,256]{1,0:T(8,128)} async-done(((f32[256,256]{1,0:T(8,128)}), f32[256,256]{1,0:T(8,128)}) %all-reduce.20.cloned.1.call-update) | async-done | bytes 262160 | tf_op jit(solution)/shard_map/psum | solution.py:133
  1170.0 49.2 %all-reduce.18.cloned.1.call-done = f32[256,2048]{1,0:T(8,128)} async-done(((f32[256,2048]{1,0:T(8,128)}), f32[256,2048]{1,0:T(8,128)}) %all-reduce.18.cloned.1.call-update) | async-done | bytes 2097168 | tf_op jit(solution)/shard_map/psum | solution.py:132
  1225.2 5.5 collective-permute-start.14
  1233.0 67.1 %collective-permute-done.14 = f32[128,2048]{1,0:T(8,128)} collective-permute-done((f32[128,2048]{1,0:T(8,128)S(1)}, f32[128,2048]{1,0:T(8,128)}, u32[]{:S(2)}, u32[]{:S(2)}) %collective-permute-start.14) | collective-permute-done | bytes 1048608 | tf_op jit(solution)/shard_map/ppermute | solution.py:60
  1301.7 20.6 %collective-permute-done.12 = f32[128,2048]{1,0:T(8,128)} collective-permute-done((f32[128,2048]{1,0:T(8,128)S(1)}, f32[128,2048]{1,0:T(8,128)}, u32[]{:S(2)}, u32[]{:S(2)}) %collective-permute-start.12) | collective-permute-done | bytes 1048608 | tf_op jit(solution)/shard_map/ppermute | solution.py:60
  1323.8 47.2 %fusion = f32[4096,2048]{1,0:T(8,128)} fusion(f32[256,4096]{1,0:T(8,128)S(1)} %copy-done.3, f32[128,2048]{1,0:T(8,128)} %copy-done.14, f32[128,2048]{1,0:T(8,128)S(1)} %copy-done.13, f32[128,2048]{1,0:T(8,128)} %copy-done.16, f32[128,2048]{1,0:T(8,128)} %copy-done.15, f32[256,4096]{1,0:T(8,128)S(1)} %copy-done.1, f32[256,2048]{1,0:T(8,128)S(1)} %fusion.37, ...), kind=kOutput, calls=%fused_computation.9 | convolution fusion | flops 38673580032 | bytes 52428800 | tf_op jit(solution)/shard_map/dot_general | solution.py:13
  1377.0 42.6 %subtract_subtract_fusion = f32[4096,2048]{1,0:T(8,128)} fusion(f32[4096,2048]{1,0:T(8,128)} %param.4, f32[4096,2048]{1,0:T(8,128)} %fusion, f32[256,2048]{1,0:T(8,128)S(1)} %copy-done.6, f32[128,2048]{1,0:T(8,128)} %get-tuple-element.90, f32[128,2048]{1,0:T(8,128)S(1)} %get-tuple-element.89, f32[128,2048]{1,0:T(8,128)} %get-tuple-element.86, ...), kind=kOutput, calls=%fused_computation.8 | convolution fusion | flops 12904824832 | bytes 106954752 | tf_op jit(solution)/shard_map/dot_general | solution.py:13
  (242 shorter events, 147.4 us)
Async XLA Ops:
  6.5 142.4 %all-reduce.10.cloned.1.call-start = ((), (), s32[]{:S(2)}) async-start(), calls=%async_computation | async-start | bytes 1048576 | tf_op jit(solution)/shard_map/psum | solution.py:103
  6.5 18.0 %copy-start.26 = (pred[4096]{0:T(1024)(128)(4,1)}, pred[4096]{0:T(1024)(128)(4,1)S(1)}, u32[]{:S(2)}) copy-start(pred[4096]{0:T(1024)(128)(4,1)S(1)} %fusion.99) | copy-start | bytes 12292
  19.8 215.7 %all-reduce.12.cloned.1.call-start = ((), (), s32[]{:S(2)}) async-start(), calls=%async_computation.1 | async-start | bytes 4194304 | tf_op jit(solution)/shard_map/psum | solution.py:94
  24.6 496.2 %all-reduce.14.cloned.1.call-start = ((), (), s32[]{:S(2)}) async-start(), calls=%async_computation.2 | async-start | bytes 1048576 | tf_op jit(solution)/shard_map/psum | solution.py:114
  149.0 63.5 %copy-start.18 = (f32[512,256]{1,0:T(8,128)S(1)}, f32[512,256]{1,0:T(8,128)}, u32[]{:S(2)}) copy-start(f32[512,256]{1,0:T(8,128)} %all-reduce.10.cloned.1.call-done) | copy-start | bytes 1572868
  238.2 72.7 %collective-permute-start.2 = (f32[128,2048]{1,0:T(8,128)}, f32[128,2048]{1,0:T(8,128)}, u32[]{:S(2)}, u32[]{:S(2)}) collective-permute-start(f32[128,2048]{1,0:T(8,128)} %get-tuple-element.106), channel_id=1, source_target_pairs={{0,0},{4,4},{8,1},{12,5},{16,2},{20,6},{24,3},{28,7},{1,8},{5,12},... | collective-permute-start | bytes 3145736 | tf_op jit(solution)/shard_map/ppermute | solution.py:60
  256.5 79.7 %collective-permute-start = (f32[128,2048]{1,0:T(8,128)S(1)}, f32[128,2048]{1,0:T(8,128)}, u32[]{:S(2)}, u32[]{:S(2)}) collective-permute-start(f32[128,2048]{1,0:T(8,128)S(1)} %get-tuple-element.105), channel_id=1, source_target_pairs={{0,0},{4,4},{8,1},{12,5},{16,2},{20,6},{24,3},{28,7},{1,8},{5,12},... | collective-permute-start | bytes 3145736 | tf_op jit(solution)/shard_map/ppermute | solution.py:60
  310.9 30.0 %collective-permute-start.3 = (f32[128,2048]{1,0:T(8,128)}, f32[128,2048]{1,0:T(8,128)}, u32[]{:S(2)}, u32[]{:S(2)}) collective-permute-start(f32[128,2048]{1,0:T(8,128)} %collective-permute-done.2), channel_id=1, source_target_pairs={{0,4},{4,0},{8,12},{12,8},{16,20},{20,16},{24,28},{28,24},{1,5},{5... | collective-permute-start | bytes 3145736 | tf_op jit(solution)/shard_map/ppermute | solution.py:68
  316.2 21.1 %copy-start.29 = (s32[2,2]{1,0:T(2,128)}, s32[2,2]{1,0:T(2,128)S(1)}, u32[]{:S(2)}) copy-start(s32[2,2]{1,0:T(2,128)S(1)} %get-tuple-element.357) | copy-start | bytes 52
  336.2 15.1 %collective-permute-start.1 = (f32[128,2048]{1,0:T(8,128)}, f32[128,2048]{1,0:T(8,128)S(1)}, u32[]{:S(2)}, u32[]{:S(2)}) collective-permute-start(f32[128,2048]{1,0:T(8,128)} %collective-permute-done), channel_id=1, source_target_pairs={{0,4},{4,0},{8,12},{12,8},{16,20},{20,16},{24,28},{28,24},{1,5},{5... | collective-permute-start | bytes 3145736 | tf_op jit(solution)/shard_map/ppermute | solution.py:68
  340.9 11.8 copy-start.23
  340.9 11.8 copy-start.27
  340.9 11.8 copy-start.28
  386.5 220.4 %all-reduce.22.cloned.1.call-start = ((), (), s32[]{:S(2)}) async-start(), calls=%async_computation.6 | async-start | bytes 8388608 | tf_op jit(solution)/shard_map/psum | solution.py:112
  388.2 397.4 %all-reduce.16.cloned.1.call-start = ((), (), s32[]{:S(2)}) async-start(), calls=%async_computation.3 | async-start | bytes 1048576 | tf_op jit(solution)/shard_map/psum | solution.py:123
  606.9 3.7 copy-start.17
  614.6 3.7 copy-start.7
  621.6 273.7 %collective-permute-start.6 = (f32[128,2048]{1,0:T(8,128)}, f32[128,2048]{1,0:T(8,128)}, u32[]{:S(2)}, u32[]{:S(2)}) collective-permute-start(f32[128,2048]{1,0:T(8,128)} %get-tuple-element.100), channel_id=1, source_target_pairs={{0,0},{4,4},{8,1},{12,5},{16,2},{20,6},{24,3},{28,7},{1,8},{5,12},... | collective-permute-start | bytes 3145736 | tf_op jit(solution)/shard_map/ppermute | solution.py:60
  626.9 295.3 %collective-permute-start.4 = (f32[128,2048]{1,0:T(8,128)}, f32[128,2048]{1,0:T(8,128)}, u32[]{:S(2)}, u32[]{:S(2)}) collective-permute-start(f32[128,2048]{1,0:T(8,128)} %get-tuple-element.99), channel_id=1, source_target_pairs={{0,0},{4,4},{8,1},{12,5},{16,2},{20,6},{24,3},{28,7},{1,8},{5,12},... | collective-permute-start | bytes 3145736 | tf_op jit(solution)/shard_map/ppermute | solution.py:60
  630.3 537.1 %all-reduce.20.cloned.1.call-start = ((), (), s32[]{:S(2)}) async-start(), calls=%async_computation.5 | async-start | bytes 524288 | tf_op jit(solution)/shard_map/psum | solution.py:133
  633.4 295.9 %collective-permute-start.10 = (f32[128,2048]{1,0:T(8,128)}, f32[128,2048]{1,0:T(8,128)}, u32[]{:S(2)}, u32[]{:S(2)}) collective-permute-start(f32[128,2048]{1,0:T(8,128)} %get-tuple-element.94), channel_id=1, source_target_pairs={{0,0},{4,4},{8,1},{12,5},{16,2},{20,6},{24,3},{28,7},{1,8},{5,12},... | collective-permute-start | bytes 3145736 | tf_op jit(solution)/shard_map/ppermute | solution.py:60
  638.7 291.5 %collective-permute-start.8 = (f32[128,2048]{1,0:T(8,128)}, f32[128,2048]{1,0:T(8,128)}, u32[]{:S(2)}, u32[]{:S(2)}) collective-permute-start(f32[128,2048]{1,0:T(8,128)} %get-tuple-element.93), channel_id=1, source_target_pairs={{0,0},{4,4},{8,1},{12,5},{16,2},{20,6},{24,3},{28,7},{1,8},{5,12},... | collective-permute-start | bytes 3145736 | tf_op jit(solution)/shard_map/ppermute | solution.py:60
  824.1 100.3 %copy-start.25 = (s32[256]{0:T(256)S(1)}, s32[256]{0:T(256)}, u32[]{:S(2)}) copy-start(s32[256]{0:T(256)} %iota_add_fusion.2) | copy-start | bytes 3076
  895.3 36.1 %collective-permute-start.7 = (f32[128,2048]{1,0:T(8,128)}, f32[128,2048]{1,0:T(8,128)}, u32[]{:S(2)}, u32[]{:S(2)}) collective-permute-start(f32[128,2048]{1,0:T(8,128)} %collective-permute-done.6), channel_id=1, source_target_pairs={{0,4},{4,0},{8,12},{12,8},{16,20},{20,16},{24,28},{28,24},{1,5},{5... | collective-permute-start | bytes 3145736 | tf_op jit(solution)/shard_map/ppermute | solution.py:68
  922.2 26.3 %collective-permute-start.5 = (f32[128,2048]{1,0:T(8,128)}, f32[128,2048]{1,0:T(8,128)S(1)}, u32[]{:S(2)}, u32[]{:S(2)}) collective-permute-start(f32[128,2048]{1,0:T(8,128)} %collective-permute-done.4), channel_id=1, source_target_pairs={{0,4},{4,0},{8,12},{12,8},{16,20},{20,16},{24,28},{28,24},{1,5},{5... | collective-permute-start | bytes 3145736 | tf_op jit(solution)/shard_map/ppermute | solution.py:68
  929.3 41.7 %collective-permute-start.11 = (f32[128,2048]{1,0:T(8,128)}, f32[128,2048]{1,0:T(8,128)S(1)}, u32[]{:S(2)}, u32[]{:S(2)}) collective-permute-start(f32[128,2048]{1,0:T(8,128)} %collective-permute-done.10), channel_id=1, source_target_pairs={{0,4},{4,0},{8,12},{12,8},{16,20},{20,16},{24,28},{28,24},{1,5},{5... | collective-permute-start | bytes 3145736 | tf_op jit(solution)/shard_map/ppermute | solution.py:68
  930.3 60.4 %collective-permute-start.9 = (f32[128,2048]{1,0:T(8,128)}, f32[128,2048]{1,0:T(8,128)S(1)}, u32[]{:S(2)}, u32[]{:S(2)}) collective-permute-start(f32[128,2048]{1,0:T(8,128)} %collective-permute-done.8), channel_id=1, source_target_pairs={{0,4},{4,0},{8,12},{12,8},{16,20},{20,16},{24,28},{28,24},{1,5},{5... | collective-permute-start | bytes 3145736 | tf_op jit(solution)/shard_map/ppermute | solution.py:68
  933.1 20.9 %copy-start.12 = (f32[128,2048]{1,0:T(8,128)}, f32[128,2048]{1,0:T(8,128)S(1)}, u32[]{:S(2)}) copy-start(f32[128,2048]{1,0:T(8,128)S(1)} %get-tuple-element.101) | copy-start | bytes 3145732
  933.1 20.9 %copy-start.14 = (f32[128,2048]{1,0:T(8,128)}, f32[128,2048]{1,0:T(8,128)S(1)}, u32[]{:S(2)}) copy-start(f32[128,2048]{1,0:T(8,128)S(1)} %get-tuple-element.102) | copy-start | bytes 3145732
  949.9 4.1 copy-start.15
  950.0 4.1 copy-start.16
  954.1 38.0 %copy-start.10 = (f32[256,4096]{1,0:T(8,128)S(1)}, f32[256,4096]{1,0:T(8,128)}, u32[]{:S(2)}) copy-start(f32[256,4096]{1,0:T(8,128)} %fusion.134) | copy-start | bytes 12582916
  954.1 38.0 %copy-start.24 = (s32[4096]{0:T(1024)S(1)}, s32[4096]{0:T(1024)}, u32[]{:S(2)}) copy-start(s32[4096]{0:T(1024)} %iota_add_fusion) | copy-start | bytes 49156
  1020.8 7.1 copy-start
  1020.8 7.1 copy-start.2
  1036.8 6.0 copy-start.22
  1042.1 177.2 %all-reduce.18.cloned.1.call-start = ((), (), s32[]{:S(2)}) async-start(), calls=%async_computation.4 | async-start | bytes 4194304 | tf_op jit(solution)/shard_map/psum | solution.py:132
  1219.2 3.7 copy-start.5
  1219.2 3.7 copy-start.19
  1219.3 104.5 %copy-start.13 = (f32[128,2048]{1,0:T(8,128)S(1)}, f32[128,2048]{1,0:T(8,128)}, u32[]{:S(2)}) copy-start(f32[128,2048]{1,0:T(8,128)} %copy-done.12) | copy-start | bytes 3145732
  1222.9 100.8 %copy-start.1 = (f32[256,4096]{1,0:T(8,128)S(1)}, f32[256,4096]{1,0:T(8,128)}, u32[]{:S(2)}) copy-start(f32[256,4096]{1,0:T(8,128)} %convolution_subtract_fusion.1) | copy-start | bytes 12582916
  1223.0 100.8 %copy-start.3 = (f32[256,4096]{1,0:T(8,128)S(1)}, f32[256,4096]{1,0:T(8,128)}, u32[]{:S(2)}) copy-start(f32[256,4096]{1,0:T(8,128)} %convolution_subtract_fusion) | copy-start | bytes 12582916
  1223.0 100.8 %copy-start.9 = (f32[256,2048]{1,0:T(8,128)S(1)}, f32[256,2048]{1,0:T(8,128)}, u32[]{:S(2)}) copy-start(f32[256,2048]{1,0:T(8,128)} %copy-done.7) | copy-start | bytes 6291460
  1225.2 74.9 %collective-permute-start.14 = (f32[128,2048]{1,0:T(8,128)S(1)}, f32[128,2048]{1,0:T(8,128)}, u32[]{:S(2)}, u32[]{:S(2)}) collective-permute-start(f32[128,2048]{1,0:T(8,128)S(1)} %get-tuple-element.88), channel_id=1, source_target_pairs={{0,0},{4,4},{8,1},{12,5},{16,2},{20,6},{24,3},{28,7},{1,8},{5,12},... | collective-permute-start | bytes 3145736 | tf_op jit(solution)/shard_map/ppermute | solution.py:60
  1230.7 91.5 %collective-permute-start.12 = (f32[128,2048]{1,0:T(8,128)S(1)}, f32[128,2048]{1,0:T(8,128)}, u32[]{:S(2)}, u32[]{:S(2)}) collective-permute-start(f32[128,2048]{1,0:T(8,128)S(1)} %get-tuple-element.87), channel_id=1, source_target_pairs={{0,0},{4,4},{8,1},{12,5},{16,2},{20,6},{24,3},{28,7},{1,8},{5,12},... | collective-permute-start | bytes 3145736 | tf_op jit(solution)/shard_map/ppermute | solution.py:60
  1300.1 70.9 %collective-permute-start.15 = (f32[128,2048]{1,0:T(8,128)}, f32[128,2048]{1,0:T(8,128)}, u32[]{:S(2)}, u32[]{:S(2)}) collective-permute-start(f32[128,2048]{1,0:T(8,128)} %collective-permute-done.14), channel_id=1, source_target_pairs={{0,4},{4,0},{8,12},{12,8},{16,20},{20,16},{24,28},{28,24},{1,5},{5... | collective-permute-start | bytes 3145736 | tf_op jit(solution)/shard_map/ppermute | solution.py:68
  1322.3 51.5 %collective-permute-start.13 = (f32[128,2048]{1,0:T(8,128)}, f32[128,2048]{1,0:T(8,128)}, u32[]{:S(2)}, u32[]{:S(2)}) collective-permute-start(f32[128,2048]{1,0:T(8,128)} %collective-permute-done.12), channel_id=1, source_target_pairs={{0,4},{4,0},{8,12},{12,8},{16,20},{20,16},{24,28},{28,24},{1,5},{5... | collective-permute-start | bytes 3145736 | tf_op jit(solution)/shard_map/ppermute | solution.py:68
  1371.0 6.0 copy-start.6
  (5 other events, 11.0 us)
Sparse Core Ops, SparseCore 0:
  19.9 129.0 all-reduce.9
  151.4 49.4 all-reduce.11
  386.6 134.0 all-reduce.13
  523.2 83.6 all-reduce.21
  630.4 155.0 all-reduce.15
  1042.2 125.1 all-reduce.19
  1169.9 49.3 all-reduce.17

commit v2 on v1

--- a/solution.py
+++ b/solution.py
@@ -76,6 +76,53 @@
     return jnp.concatenate(out, axis=0)
 
 
+def exchange(block, axis, bit):
+    size = lax.axis_size(axis)
+    return lax.ppermute(block, axis, [(k, k ^ bit) for k in range(size)])
+
+
+def scatter_over_rows(block):
+    bit = 1
+    while bit < lax.axis_size("row"):
+        upper = (lax.axis_index("row") & bit) != 0
+        half = block.shape[0] // 2
+        low, top = block[:half], block[half:]
+        sent = exchange(jnp.where(upper, low, top), "row", bit)
+        block = jnp.where(upper, top, low) + sent
+        bit *= 2
+    return block
+
+
+def sum_over_cols(block):
+    bit = 1
+    while bit < lax.axis_size("col"):
+        block = block + exchange(block, "col", bit)
+        bit *= 2
+    return block
+
+
+def gather_over_rows(block):
+    bit = lax.axis_size("row") // 2
+    while bit:
+        upper = (lax.axis_index("row") & bit) != 0
+        other = exchange(block, "row", bit)
+        block = jnp.where(
+            upper, jnp.concatenate([other, block]), jnp.concatenate([block, other])
+        )
+        bit //= 2
+    return block
+
+
+def own_part(block):
+    bit = 1
+    while bit < lax.axis_size("row"):
+        upper = (lax.axis_index("row") & bit) != 0
+        half = block.shape[0] // 2
+        block = jnp.where(upper, block[half:], block[:half])
+        bit *= 2
+    return block
+
+
 def unit_rows(ids, first_row):
     return (jnp.arange(NB, dtype=jnp.int32)[:, None] + first_row == ids[None, :]).astype(jnp.float32)
 
@@ -91,7 +138,7 @@
     high = lax.Precision.HIGH
 
     def from_first_row(block):
-        return lax.psum(jnp.where(row_pos == 0, block, 0.0), "row")
+        return gather_over_rows(scatter_over_rows(jnp.where(row_pos == 0, block, 0.0)))
 
     def columns_of(block, first):
         start = first % col_block
@@ -100,37 +147,41 @@
     first_c = from_first_row(matrix[:NB])
     panel = jnp.where((row_ids >= NB)[:, None], matrix[:, :NB], 0.0)
     top = jnp.where(row_pos == 0, matrix[NB : 2 * NB, :NB], 0.0)
-    sums = lax.psum(jnp.where(col_pos == 0, jnp.concatenate([tn(panel, panel), top]), 0.0), BOTH)
+    sums = jnp.concatenate([tn(panel, panel), top.T], axis=1)
+    sums = scatter_over_rows(jnp.where(col_pos == 0, sums, 0.0))
+    sums = gather_over_rows(sum_over_cols(sums))
     first_r = to_rows(first_c, rows, ratio)
     second_c = from_first_row(lax.optimization_barrier((matrix[NB : 2 * NB], first_c))[0])
     second_r = to_rows(lax.optimization_barrier((second_c, first_r))[0], rows, ratio)
 
-    inv, basis_top, coupling = small_factors(sums[:NB], sums[NB:])
+    inv, basis_top, coupling = small_factors(sums[:, :NB], sums[:, NB:].T)
     v1_r = unit_rows(row_ids, NB) - nn(inv, jnp.where(row_ids >= NB, first_r, 0.0))
     v1_c = unit_rows(col_ids, NB) - nn(inv, jnp.where(col_ids >= NB, first_c, 0.0))
     partial = nn(v1_r, matrix, high)
-    z_c = lax.psum(partial, "row")
     z_top = columns_of(partial, NB)
-    sums = lax.psum(jnp.concatenate([nt(v1_c, partial), z_top]), BOTH)
+    sums = scatter_over_rows(jnp.concatenate([nt(v1_c, partial), z_top, partial], axis=1))
+    z_c = gather_over_rows(sums[:, 2 * NB :])
+    sums = gather_over_rows(sum_over_cols(sums[:, : 2 * NB]))
     v1_top = jnp.eye(NB, dtype=jnp.float32) - basis_top
-    inner = nn(tn(coupling, sums[:NB]), coupling)
-    s1_top = tn(sums[NB:], coupling) - 0.5 * nn(v1_top, inner)
+    inner = nn(tn(coupling, sums[:, :NB]), coupling)
+    s1_top = tn(sums[:, NB:], coupling) - 0.5 * nn(v1_top, inner)
     s1_c = tn(coupling, z_c) - 0.5 * tn(inner, v1_c)
 
     p2_c = second_c - nn(s1_top, v1_c) - nn(v1_top, s1_c)
     p2_c = jnp.where(col_ids >= 2 * NB, p2_c, 0.0)
-    top = columns_of(p2_c, 2 * NB).T
-    sums = lax.psum(jnp.concatenate([nt(p2_c, p2_c), top]), "col")
+    sums = jnp.concatenate([nt(own_part(p2_c), p2_c), own_part(columns_of(p2_c, 2 * NB))], axis=1)
+    sums = gather_over_rows(sum_over_cols(sums))
     s1_r = to_rows(s1_c, rows, ratio)
     p2_r = second_r - nn(s1_top, v1_r) - nn(v1_top, s1_r)
     p2_r = jnp.where(row_ids >= 2 * NB, p2_r, 0.0)
 
-    inv, basis_top, coupling = small_factors(sums[:NB], sums[NB:])
+    inv, basis_top, coupling = small_factors(sums[:, :NB], sums[:, NB:].T)
     v2_r = unit_rows(row_ids, 2 * NB) - nn(inv, p2_r)
     v2_c = unit_rows(col_ids, 2 * NB) - nn(inv, p2_c)
     partial = nn(v2_r, matrix, high) - nn(nt(v2_r, s1_r), v1_c) - nn(nt(v2_r, v1_r), s1_c)
-    z_c = lax.psum(partial, "row")
-    inner = lax.psum(nt(v2_c, partial), BOTH)
+    sums = scatter_over_rows(jnp.concatenate([nt(v2_c, partial), partial], axis=1))
+    z_c = gather_over_rows(sums[:, NB:])
+    inner = gather_over_rows(sum_over_cols(sums[:, :NB]))
     inner = nn(tn(coupling, inner), coupling)
     s2_c = tn(coupling, z_c) - 0.5 * tn(inner, v2_c)
     s2_r = to_rows(s2_c, rows, ratio)

time: 1440 us -> 957 us (0.66)
  waiting for transfers between devices: 841 us -> 271 us
  starting transfers between devices: 40.8 us -> 101 us
  other arithmetic: 251 us -> 286 us
    psum x7 -> x0, waiting for transfers between devices: 644 us -> none  [the longest x1 144 us: shards(): sums = lax.psum(jnp.concatenate([nt(p2_c, p2_c), top]), 'col')]
    ppermute x0 -> x38, waiting for transfers between devices: none -> 76.6 us  [exchange(): return lax.ppermute(block, axis, [(k, k ^ bit) for k in range(size)])]
    ppermute x0 -> x38, starting transfers between devices: none -> 51.4 us  [exchange(): return lax.ppermute(block, axis, [(k, k ^ bit) for k in range(size)])]
    ppermute x8, waiting for transfers between devices: 59.2 us -> 22.1 us  [to_rows(): parts.append(lax.ppermute(own, 'col', turn))]
    ppermute x8, waiting for transfers between devices: 138 us -> 172 us  [to_rows(): own = lax.ppermute(block[chunk * height:(chunk + 1) * height], BOTH, swap)]
  transfers between devices with their start and end apart: 23 -> 54, of which waited for: 13 -> 23; matrix products, arithmetic and copies ran while one was open for 25% -> 46% of each run, Pallas kernels for 0% -> 0%
where the time goes in v2:
time: 957 us; the launch traced here: 943 us
  other arithmetic  286 us (30%)
  waiting for transfers between devices  271 us (28%)
  matrix products  237 us (25%)
  starting transfers between devices  101 us (11%)
  local copies, waits for them, and re-layouts  41.5 us (4%)
    dot_general x38, matrix products, mm(): lax.dot_general(left, right, ((dims[0], dims[1]), ((), ())), precision=pr...  222 us
    ppermute x8, waiting for transfers between devices, to_rows(): own = lax.ppermute(block[chunk * height:(chunk + 1) * height], BOTH, swap)  172 us
    another operation x27, other arithmetic, inverse_factor(): lower = jnp.linalg.cholesky(gram)  146 us
    another operation x9, other arithmetic, inverse_factor(): return lax.linalg.triangular_solve(lower, eye, left_side=True, lower=True)  85.8 us
    ppermute x38, waiting for transfers between devices, exchange(): return lax.ppermute(block, axis, [(k, k ^ bit) for k in range(size)])  76.6 us
    ppermute x38, starting transfers between devices, exchange(): return lax.ppermute(block, axis, [(k, k ^ bit) for k in range(size)])  51.4 us
    ppermute x8, starting transfers between devices, to_rows(): own = lax.ppermute(block[chunk * height:(chunk + 1) * height], BOTH, swap)  39.5 us
    another operation x29, local copies, waits for them, and re-layouts, inverse_factor(): return lax.linalg.triangular_solve(lower, eye, left_side=True, lower=True)  22.6 us
  transfers between devices with their start and end apart: 54, of which 23 were waited for; matrix products, arithmetic and copies ran while one was open for 46% of the time, Pallas kernels for 0%

profile of v2, /device:TPU:2, one launch (start us, length us, event | category | flops | bytes accessed | tf_op | source)
XLA Modules:
  0.0 943.4 jit_solution(12885724407619632719)
XLA Ops:
  1.1 11.3 %fusion.34 = f32[256,256]{1,0:T(8,128)S(1)} fusion(f32[4096,2048]{1,0:T(8,128)} %param.4, pred[4096]{0:T(1024)(128)(4,1)S(1)} %fusion.119), kind=kOutput, calls=%fused_computation.47 | convolution fusion | flops 3222274048 | bytes 4460544 | tf_op jit(solution)/shard_map/dot_general | solution.py:13
  17.6 5.2 collective-permute-done.1
  49.8 12.1 %cholesky.214 = f32[128,128]{1,0:T(8,128)S(1)} custom-call(f32[128,128]{1,0:T(8,128)S(1)} %copy.5), custom_call_target="Cholesky" | custom-call | tf_op jit(solution)/shard_map/jit(cholesky)/cholesky | solution.py:35
  61.9 9.8 %custom-call.17 = f32[1,128,128]{1,2,0:T(8,128)S(1)} custom-call(f32[1,128,128]{2,1,0:T(8,128)S(1)} %get-tuple-element.122), custom_call_target="InvertDiagBlocksLowerTriangular" | custom-call | tf_op jit(solution)/shard_map/jit(cholesky)/cholesky | solution.py:35
  72.4 11.7 %cholesky.231 = f32[128,128]{1,0:T(8,128)S(1)} custom-call(f32[128,128]{1,0:T(8,128)S(1)} %copy.7), custom_call_target="Cholesky" | custom-call | tf_op jit(solution)/shard_map/jit(cholesky)/cholesky | solution.py:35
  92.3 19.7 %custom-call.18 = f32[2,128,128]{1,2,0:T(8,128)S(1)} custom-call(f32[2,128,128]{2,1,0:T(8,128)S(1)} %get-tuple-element.37), custom_call_target="InvertDiagBlocksLowerTriangular" | custom-call | tf_op jit(solution)/shard_map/triangular_solve/custom-call.0 | solution.py:37
  122.6 4.6 collective-permute-start.11
  129.8 11.7 %cholesky.248 = f32[128,128]{1,0:T(8,128)S(1)} custom-call(f32[128,128]{1,0:T(8,128)S(1)} %cholesky.349), custom_call_target="Cholesky" | custom-call | tf_op jit(solution)/shard_map/jit(cholesky)/cholesky | solution.py:35
  141.5 9.8 %custom-call.19 = f32[1,128,128]{1,2,0:T(8,128)S(1)} custom-call(f32[1,128,128]{2,1,0:T(8,128)S(1)} %get-tuple-element.118), custom_call_target="InvertDiagBlocksLowerTriangular" | custom-call | tf_op jit(solution)/shard_map/jit(cholesky)/cholesky | solution.py:35
  151.9 12.3 %cholesky.265 = f32[128,128]{1,0:T(8,128)} custom-call(f32[128,128]{1,0:T(8,128)S(1)} %convolution_subtract_fusion.17), custom_call_target="Cholesky" | custom-call | tf_op jit(solution)/shard_map/jit(cholesky)/cholesky | solution.py:35
  164.9 29.3 %collective-permute-done.13 = f32[128,2048]{1,0:T(8,128)} collective-permute-done((f32[128,2048]{1,0:T(8,128)}, f32[128,2048]{1,0:T(8,128)}, u32[]{:S(2)}, u32[]{:S(2)}) %collective-permute-start.13) | collective-permute-done | bytes 1048608 | tf_op jit(solution)/shard_map/ppermute | solution.py:60
  199.7 15.8 %collective-permute-done.11 = f32[128,2048]{1,0:T(8,128)} collective-permute-done((f32[128,2048]{1,0:T(8,128)}, f32[128,2048]{1,0:T(8,128)}, u32[]{:S(2)}, u32[]{:S(2)}) %collective-permute-start.11) | collective-permute-done | bytes 1048608 | tf_op jit(solution)/shard_map/ppermute | solution.py:60
  220.9 9.7 %collective-permute-done.12 = f32[128,2048]{1,0:T(8,128)S(1)} collective-permute-done((f32[128,2048]{1,0:T(8,128)}, f32[128,2048]{1,0:T(8,128)S(1)}, u32[]{:S(2)}, u32[]{:S(2)}) %collective-permute-start.12) | collective-permute-done | bytes 1048608 | tf_op jit(solution)/shard_map/ppermute | solution.py:68
  232.0 7.4 convolution_subtract_fusion.1
  239.4 20.6 %fusion.153 = f32[256,2048]{1,0:T(8,128)} fusion(f32[256,4096]{1,0:T(8,128)} %convolution_subtract_fusion.1, f32[4096,2048]{1,0:T(8,128)} %param.4), kind=kOutput, calls=%fused_computation.314 | convolution fusion | flops 12884901888 | bytes 39845888 | tf_op jit(solution)/shard_map/dot_general | solution.py:13
  274.7 11.6 %collective-permute-done.30 = f32[64,2048]{1,0:T(8,128)S(1)} collective-permute-done((f32[64,2048]{1,0:T(8,128)}, f32[64,2048]{1,0:T(8,128)S(1)}, u32[]{:S(2)}, u32[]{:S(2)}) %collective-permute-start.30) | collective-permute-done | bytes 524320 | tf_op jit(solution)/shard_map/ppermute | solution.py:81
  291.4 5.8 while.9
  297.8 20.5 %custom-call.20 = f32[2,128,128]{1,2,0:T(8,128)S(1)} custom-call(f32[2,128,128]{2,1,0:T(8,128)} %copy-done.56), custom_call_target="InvertDiagBlocksLowerTriangular" | custom-call | tf_op jit(solution)/shard_map/triangular_solve/custom-call.0 | solution.py:37
  326.1 12.9 %collective-permute-start.39 = (f32[128,2048]{1,0:T(8,128)S(1)}, f32[128,2048]{1,0:T(8,128)}, u32[]{:S(2)}, u32[]{:S(2)}) collective-permute-start(f32[128,2048]{1,0:T(8,128)S(1)} %get-tuple-element.92), channel_id=1, source_target_pairs={{0,0},{4,4},{8,1},{12,5},{16,2},{20,6},{24,3},{28,7},{1,8},{5,12},... | collective-permute-start | bytes 3145736 | tf_op jit(solution)/shard_map/ppermute | solution.py:60
  340.6 14.4 %collective-permute-done.20 = f32[64,512]{1,0:T(8,128)S(1)} collective-permute-done((f32[64,512]{1,0:T(8,128)S(1)}, f32[64,512]{1,0:T(8,128)S(1)}, u32[]{:S(2)}, u32[]{:S(2)}) %collective-permute-start.20) | collective-permute-done | bytes 131104 | tf_op jit(solution)/shard_map/ppermute | solution.py:81
  356.8 5.3 collective-permute-start.17
  362.1 22.9 %collective-permute-start.22 = (f32[64,512]{1,0:T(8,128)S(1)}, f32[64,512]{1,0:T(8,128)S(1)}, u32[]{:S(2)}, u32[]{:S(2)}) collective-permute-start(f32[64,512]{1,0:T(8,128)S(1)} %add.176), channel_id=1, source_target_pairs={{0,2},{1,3},{2,0},{3,1},{4,6},{5,7},{6,4},{7,5},{8,10},{9,11},{10,... | collective-permute-start | bytes 393224 | tf_op jit(solution)/shard_map/ppermute | solution.py:81
  411.9 27.2 %collective-permute-done.37 = f32[128,2048]{1,0:T(8,128)} collective-permute-done((f32[128,2048]{1,0:T(8,128)}, f32[128,2048]{1,0:T(8,128)}, u32[]{:S(2)}, u32[]{:S(2)}) %collective-permute-start.37) | collective-permute-done | bytes 1048608 | tf_op jit(solution)/shard_map/ppermute | solution.py:60
  440.7 8.2 fusion.156
  452.1 10.2 %collective-permute-done.34 = f32[64,512]{0,1:T(8,128)S(1)} collective-permute-done((f32[64,512]{0,1:T(8,128)S(1)}, f32[64,512]{0,1:T(8,128)S(1)}, u32[]{:S(2)}, u32[]{:S(2)}) %collective-permute-start.34) | collective-permute-done | bytes 131104 | tf_op jit(solution)/shard_map/ppermute | solution.py:81
  465.4 5.3 collective-permute-done.35
  474.4 5.7 collective-permute-start.24
  482.8 11.7 %cholesky.282 = f32[128,128]{1,0:T(8,128)S(1)} custom-call(f32[128,128]{1,0:T(8,128)S(1)} %cholesky.352), custom_call_target="Cholesky" | custom-call | tf_op jit(solution)/shard_map/jit(cholesky)/cholesky | solution.py:35
  495.1 10.4 %custom-call.21 = f32[1,128,128]{1,2,0:T(8,128)} custom-call(f32[1,128,128]{2,1,0:T(8,128)S(1)} %get-tuple-element.114), custom_call_target="InvertDiagBlocksLowerTriangular" | custom-call | tf_op jit(solution)/shard_map/jit(cholesky)/cholesky | solution.py:35
  507.7 11.7 %cholesky.299 = f32[128,128]{1,0:T(8,128)S(1)} custom-call(f32[128,128]{1,0:T(8,128)S(1)} %convolution_subtract_fusion.16), custom_call_target="Cholesky" | custom-call | tf_op jit(solution)/shard_map/jit(cholesky)/cholesky | solution.py:35
  523.6 5.2 while.10
  528.8 20.4 %custom-call.22 = f32[2,128,128]{1,2,0:T(8,128)} custom-call(f32[2,128,128]{2,1,0:T(8,128)S(1)} %get-tuple-element.39), custom_call_target="InvertDiagBlocksLowerTriangular" | custom-call | tf_op jit(solution)/shard_map/triangular_solve/custom-call.0 | solution.py:37
  554.6 12.1 %collective-permute-done.24 = f32[128,2048]{1,0:T(8,128)} collective-permute-done((f32[128,2048]{1,0:T(8,128)}, f32[128,2048]{1,0:T(8,128)}, u32[]{:S(2)}, u32[]{:S(2)}) %collective-permute-start.24) | collective-permute-done | bytes 1048608 | tf_op jit(solution)/shard_map/ppermute | solution.py:60
  569.1 12.3 %cholesky.316 = f32[128,128]{1,0:T(8,128)} custom-call(f32[128,128]{1,0:T(8,128)S(1)} %cholesky.355), custom_call_target="Cholesky" | custom-call | tf_op jit(solution)/shard_map/jit(cholesky)/cholesky | solution.py:35
  581.4 5.0 convolution_subtract_fusion.5
  588.2 12.5 %collective-permute-done.25 = f32[128,2048]{1,0:T(8,128)} collective-permute-done((f32[128,2048]{1,0:T(8,128)}, f32[128,2048]{1,0:T(8,128)}, u32[]{:S(2)}, u32[]{:S(2)}) %collective-permute-start.25) | collective-permute-done | bytes 1048608 | tf_op jit(solution)/shard_map/ppermute | solution.py:68
  606.6 8.0 convolution_subtract_fusion
  614.7 21.1 %fusion.158 = f32[256,2048]{1,0:T(8,128)} fusion(f32[256,4096]{1,0:T(8,128)} %convolution_subtract_fusion, f32[4096,2048]{1,0:T(8,128)} %param.4), kind=kOutput, calls=%fused_computation.319 | convolution fusion | flops 12884901888 | bytes 39845888 | tf_op jit(solution)/shard_map/dot_general | solution.py:13
  635.8 6.8 fusion.39
  654.4 11.3 %custom-call.23 = f32[1,128,128]{1,2,0:T(8,128)} custom-call(f32[1,128,128]{2,1,0:T(8,128)} %get-tuple-element.110), custom_call_target="InvertDiagBlocksLowerTriangular" | custom-call | tf_op jit(solution)/shard_map/jit(cholesky)/cholesky | solution.py:35
  669.1 13.2 %cholesky.333 = f32[128,128]{1,0:T(8,128)} custom-call(f32[128,128]{1,0:T(8,128)} %convolution_subtract_fusion.15), custom_call_target="Cholesky" | custom-call | tf_op jit(solution)/shard_map/jit(cholesky)/cholesky | solution.py:35
  691.7 7.0 while.11
  698.7 21.3 %custom-call.24 = f32[2,128,128]{1,2,0:T(8,128)} custom-call(f32[2,128,128]{2,1,0:T(8,128)} %get-tuple-element.40), custom_call_target="InvertDiagBlocksLowerTriangular" | custom-call | tf_op jit(solution)/shard_map/triangular_solve/custom-call.0 | solution.py:37
  731.2 4.6 collective-permute-done.47
  756.1 67.1 %collective-permute-done.52 = f32[128,2048]{1,0:T(8,128)} collective-permute-done((f32[128,2048]{1,0:T(8,128)S(1)}, f32[128,2048]{1,0:T(8,128)}, u32[]{:S(2)}, u32[]{:S(2)}) %collective-permute-start.52) | collective-permute-done | bytes 1048608 | tf_op jit(solution)/shard_map/ppermute | solution.py:60
  824.7 20.7 %collective-permute-done.50 = f32[128,2048]{1,0:T(8,128)} collective-permute-done((f32[128,2048]{1,0:T(8,128)S(1)}, f32[128,2048]{1,0:T(8,128)}, u32[]{:S(2)}, u32[]{:S(2)}) %collective-permute-start.50) | collective-permute-done | bytes 1048608 | tf_op jit(solution)/shard_map/ppermute | solution.py:60
  846.9 47.3 %fusion = f32[4096,2048]{1,0:T(8,128)} fusion(f32[256,4096]{1,0:T(8,128)S(1)} %copy-done.3, f32[128,2048]{1,0:T(8,128)} %copy-done.29, f32[128,2048]{1,0:T(8,128)S(1)} %copy-done.28, f32[128,2048]{1,0:T(8,128)} %copy-done.31, f32[128,2048]{1,0:T(8,128)} %copy-done.30, f32[256,4096]{1,0:T(8,128)S(1)} %copy-done.1, ...), kind=kOutput, calls=%fused_computation.9 | convolution fusion | flops 38673580032 | bytes 52428800 | tf_op jit(solution)/shard_map/dot_general | solution.py:13
  900.2 42.7 %subtract_subtract_fusion = f32[4096,2048]{1,0:T(8,128)} fusion(f32[4096,2048]{1,0:T(8,128)} %param.4, f32[4096,2048]{1,0:T(8,128)} %fusion, f32[256,2048]{1,0:T(8,128)S(1)} %copy-done.7, f32[128,2048]{1,0:T(8,128)} %get-tuple-element.88, f32[128,2048]{1,0:T(8,128)S(1)} %get-tuple-element.87, f32[128,2048]{1,0:T(8,128)} %get-tuple-element.84, ...), kind=kOutput, calls=%fused_computation.8 | convolution fusion | flops 12904824832 | bytes 106954752 | tf_op jit(solution)/shard_map/dot_general | solution.py:13
  (432 shorter events, 244.2 us)
Async XLA Ops:
  16.9 6.0 collective-permute-start.1
  17.1 29.6 %collective-permute-start.7 = (f32[128,2048]{1,0:T(8,128)S(1)}, f32[128,2048]{1,0:T(8,128)}, u32[]{:S(2)}, u32[]{:S(2)}) collective-permute-start(f32[128,2048]{1,0:T(8,128)S(1)} %slice_select_fusion.4), channel_id=1, source_target_pairs={{0,1},{1,0},{2,3},{3,2},{4,5},{5,4},{6,7},{7,6},{8,9},{9,8},{10,11... | collective-permute-start | bytes 3145736 | tf_op jit(solution)/shard_map/ppermute | solution.py:81
  22.8 5.2 collective-permute-start.2
  28.0 5.0 collective-permute-start.3
  33.1 7.3 collective-permute-start.4
  40.5 5.1 collective-permute-start.5
  48.9 37.1 %collective-permute-start.8 = (f32[64,2048]{1,0:T(8,128)}, f32[64,2048]{1,0:T(8,128)S(1)}, u32[]{:S(2)}, u32[]{:S(2)}) collective-permute-start(f32[64,2048]{1,0:T(8,128)} %slice_select_fusion.10), channel_id=1, source_target_pairs={{0,2},{1,3},{2,0},{3,1},{4,6},{5,7},{6,4},{7,5},{8,10},{9,11},{10,... | collective-permute-start | bytes 1572872 | tf_op jit(solution)/shard_map/ppermute | solution.py:81
  86.1 25.9 %collective-permute-start.9 = (f32[64,2048]{1,0:T(8,128)S(1)}, f32[64,2048]{1,0:T(8,128)S(1)}, u32[]{:S(2)}, u32[]{:S(2)}) collective-permute-start(f32[64,2048]{1,0:T(8,128)S(1)} %select_add_fusion.7), channel_id=1, source_target_pairs={{0,2},{1,3},{2,0},{3,1},{4,6},{5,7},{6,4},{7,5},{8,10},{9,11},{10,... | collective-permute-start | bytes 1572872 | tf_op jit(solution)/shard_map/ppermute | solution.py:81
  119.3 74.9 %collective-permute-start.13 = (f32[128,2048]{1,0:T(8,128)}, f32[128,2048]{1,0:T(8,128)}, u32[]{:S(2)}, u32[]{:S(2)}) collective-permute-start(f32[128,2048]{1,0:T(8,128)} %get-tuple-element.104), channel_id=1, source_target_pairs={{0,0},{4,4},{8,1},{12,5},{16,2},{20,6},{24,3},{28,7},{1,8},{5,12},... | collective-permute-start | bytes 3145736 | tf_op jit(solution)/shard_map/ppermute | solution.py:60
  122.6 92.9 %collective-permute-start.11 = (f32[128,2048]{1,0:T(8,128)}, f32[128,2048]{1,0:T(8,128)}, u32[]{:S(2)}, u32[]{:S(2)}) collective-permute-start(f32[128,2048]{1,0:T(8,128)} %get-tuple-element.103), channel_id=1, source_target_pairs={{0,0},{4,4},{8,1},{12,5},{16,2},{20,6},{24,3},{28,7},{1,8},{5,12},... | collective-permute-start | bytes 3145736 | tf_op jit(solution)/shard_map/ppermute | solution.py:60
  128.6 88.5 %collective-permute-start.28 = (f32[128,2048]{1,0:T(8,128)}, f32[128,2048]{1,0:T(8,128)}, u32[]{:S(2)}, u32[]{:S(2)}) collective-permute-start(f32[128,2048]{1,0:T(8,128)} %slice_select_fusion.3), channel_id=1, source_target_pairs={{0,1},{1,0},{2,3},{3,2},{4,5},{5,4},{6,7},{7,6},{8,9},{9,8},{10,11... | collective-permute-start | bytes 3145736 | tf_op jit(solution)/shard_map/ppermute | solution.py:81
  194.2 25.2 %collective-permute-start.14 = (f32[128,2048]{1,0:T(8,128)}, f32[128,2048]{1,0:T(8,128)S(1)}, u32[]{:S(2)}, u32[]{:S(2)}) collective-permute-start(f32[128,2048]{1,0:T(8,128)} %collective-permute-done.13), channel_id=1, source_target_pairs={{0,4},{4,0},{8,12},{12,8},{16,20},{20,16},{24,28},{28,24},{1,5},{5... | collective-permute-start | bytes 3145736 | tf_op jit(solution)/shard_map/ppermute | solution.py:68
  215.5 15.0 %collective-permute-start.12 = (f32[128,2048]{1,0:T(8,128)}, f32[128,2048]{1,0:T(8,128)S(1)}, u32[]{:S(2)}, u32[]{:S(2)}) collective-permute-start(f32[128,2048]{1,0:T(8,128)} %collective-permute-done.11), channel_id=1, source_target_pairs={{0,4},{4,0},{8,12},{12,8},{16,20},{20,16},{24,28},{28,24},{1,5},{5... | collective-permute-start | bytes 3145736 | tf_op jit(solution)/shard_map/ppermute | solution.py:68
  219.4 50.4 %collective-permute-start.29 = (f32[64,2048]{1,0:T(8,128)}, f32[64,2048]{1,0:T(8,128)}, u32[]{:S(2)}, u32[]{:S(2)}) collective-permute-start(f32[64,2048]{1,0:T(8,128)} %slice_select_fusion.9), channel_id=1, source_target_pairs={{0,2},{1,3},{2,0},{3,1},{4,6},{5,7},{6,4},{7,5},{8,10},{9,11},{10,... | collective-permute-start | bytes 1572872 | tf_op jit(solution)/shard_map/ppermute | solution.py:81
  269.8 18.8 %collective-permute-start.15 = (f32[128,2560]{1,0:T(8,128)}, f32[128,2560]{1,0:T(8,128)}, u32[]{:S(2)}, u32[]{:S(2)}) collective-permute-start(f32[128,2560]{1,0:T(8,128)} %slice_select_fusion.1), channel_id=1, source_target_pairs={{0,1},{1,0},{2,3},{3,2},{4,5},{5,4},{6,7},{7,6},{8,9},{9,8},{10,11... | collective-permute-start | bytes 3932168 | tf_op jit(solution)/shard_map/ppermute | solution.py:81
  271.9 14.4 %collective-permute-start.30 = (f32[64,2048]{1,0:T(8,128)}, f32[64,2048]{1,0:T(8,128)S(1)}, u32[]{:S(2)}, u32[]{:S(2)}) collective-permute-start(f32[64,2048]{1,0:T(8,128)} %select_add_fusion.6), channel_id=1, source_target_pairs={{0,2},{1,3},{2,0},{3,1},{4,6},{5,7},{6,4},{7,5},{8,10},{9,11},{10,... | collective-permute-start | bytes 1572872 | tf_op jit(solution)/shard_map/ppermute | solution.py:81
  288.6 31.0 %collective-permute-start.31 = (f32[128,2048]{1,0:T(8,128)}, f32[128,2048]{1,0:T(8,128)}, u32[]{:S(2)}, u32[]{:S(2)}) collective-permute-start(f32[128,2048]{1,0:T(8,128)} %maximum_select_fusion.8), channel_id=1, source_target_pairs={{0,1},{1,0},{2,3},{3,2},{4,5},{5,4},{6,7},{7,6},{8,9},{9,8},{10,11... | collective-permute-start | bytes 3145736 | tf_op jit(solution)/shard_map/ppermute | solution.py:81
  291.1 31.0 %collective-permute-start.16 = (f32[64,2560]{1,0:T(8,128)}, f32[64,2560]{1,0:T(8,128)}, u32[]{:S(2)}, u32[]{:S(2)}) collective-permute-start(f32[64,2560]{1,0:T(8,128)} %slice_select_fusion.5), channel_id=1, source_target_pairs={{0,2},{1,3},{2,0},{3,1},{4,6},{5,7},{6,4},{7,5},{8,10},{9,11},{10,... | collective-permute-start | bytes 1966088 | tf_op jit(solution)/shard_map/ppermute | solution.py:81
  323.4 15.6 %collective-permute-start.19 = (f32[64,512]{1,0:T(8,128)S(1)}, f32[64,512]{1,0:T(8,128)S(1)}, u32[]{:S(2)}, u32[]{:S(2)}) collective-permute-start(f32[64,512]{1,0:T(8,128)S(1)} %slice.324), channel_id=1, source_target_pairs={{0,4},{4,0},{8,12},{12,8},{16,20},{20,16},{24,28},{28,24},{1,5},{5... | collective-permute-start | bytes 393224 | tf_op jit(solution)/shard_map/ppermute | solution.py:81
  326.1 66.6 %collective-permute-start.39 = (f32[128,2048]{1,0:T(8,128)S(1)}, f32[128,2048]{1,0:T(8,128)}, u32[]{:S(2)}, u32[]{:S(2)}) collective-permute-start(f32[128,2048]{1,0:T(8,128)S(1)} %get-tuple-element.92), channel_id=1, source_target_pairs={{0,0},{4,4},{8,1},{12,5},{16,2},{20,6},{24,3},{28,7},{1,8},{5,12},... | collective-permute-start | bytes 3145736 | tf_op jit(solution)/shard_map/ppermute | solution.py:60
  339.0 16.0 %collective-permute-start.20 = (f32[64,512]{1,0:T(8,128)S(1)}, f32[64,512]{1,0:T(8,128)S(1)}, u32[]{:S(2)}, u32[]{:S(2)}) collective-permute-start(f32[64,512]{1,0:T(8,128)S(1)} %slice_add_fusion.1), channel_id=1, source_target_pairs={{0,8},{4,12},{8,0},{12,4},{16,24},{20,28},{24,16},{28,20},{1,9},{5... | collective-permute-start | bytes 393224 | tf_op jit(solution)/shard_map/ppermute | solution.py:81
  355.1 7.1 collective-permute-start.21
  356.8 36.5 %collective-permute-start.17 = (f32[64,2048]{1,0:T(8,128)S(1)}, f32[64,2048]{1,0:T(8,128)S(1)}, u32[]{:S(2)}, u32[]{:S(2)}) collective-permute-start(f32[64,2048]{1,0:T(8,128)S(1)} %slice.323), channel_id=1, source_target_pairs={{0,2},{1,3},{2,0},{3,1},{4,6},{5,7},{6,4},{7,5},{8,10},{9,11},{10,... | collective-permute-start | bytes 1572872 | tf_op jit(solution)/shard_map/ppermute | solution.py:81
  362.1 26.7 %collective-permute-start.22 = (f32[64,512]{1,0:T(8,128)S(1)}, f32[64,512]{1,0:T(8,128)S(1)}, u32[]{:S(2)}, u32[]{:S(2)}) collective-permute-start(f32[64,512]{1,0:T(8,128)S(1)} %add.176), channel_id=1, source_target_pairs={{0,2},{1,3},{2,0},{3,1},{4,6},{5,7},{6,4},{7,5},{8,10},{9,11},{10,... | collective-permute-start | bytes 393224 | tf_op jit(solution)/shard_map/ppermute | solution.py:81
  388.8 4.6 collective-permute-start.23
  389.5 49.6 %collective-permute-start.37 = (f32[128,2048]{1,0:T(8,128)}, f32[128,2048]{1,0:T(8,128)}, u32[]{:S(2)}, u32[]{:S(2)}) collective-permute-start(f32[128,2048]{1,0:T(8,128)} %get-tuple-element.91), channel_id=1, source_target_pairs={{0,0},{4,4},{8,1},{12,5},{16,2},{20,6},{24,3},{28,7},{1,8},{5,12},... | collective-permute-start | bytes 3145736 | tf_op jit(solution)/shard_map/ppermute | solution.py:60
  392.7 56.3 %collective-permute-start.40 = (f32[128,2048]{1,0:T(8,128)}, f32[128,2048]{1,0:T(8,128)}, u32[]{:S(2)}, u32[]{:S(2)}) collective-permute-start(f32[128,2048]{1,0:T(8,128)} %collective-permute-done.39), channel_id=1, source_target_pairs={{0,4},{4,0},{8,12},{12,8},{16,20},{20,16},{24,28},{28,24},{1,5},{5... | collective-permute-start | bytes 3145736 | tf_op jit(solution)/shard_map/ppermute | solution.py:68
  410.0 29.7 %collective-permute-start.32 = (f32[64,512]{0,1:T(8,128)S(1)}, f32[64,512]{0,1:T(8,128)}, u32[]{:S(2)}, u32[]{:S(2)}) collective-permute-start(f32[64,512]{0,1:T(8,128)S(1)} %pad_maximum_fusion.4), channel_id=1, source_target_pairs={{0,4},{4,0},{8,12},{12,8},{16,20},{20,16},{24,28},{28,24},{1,5},{5... | collective-permute-start | bytes 393224 | tf_op jit(solution)/shard_map/ppermute | solution.py:81
  439.1 23.3 %collective-permute-start.38 = (f32[128,2048]{1,0:T(8,128)}, f32[128,2048]{1,0:T(8,128)S(1)}, u32[]{:S(2)}, u32[]{:S(2)}) collective-permute-start(f32[128,2048]{1,0:T(8,128)} %collective-permute-done.37), channel_id=1, source_target_pairs={{0,4},{4,0},{8,12},{12,8},{16,20},{20,16},{24,28},{28,24},{1,5},{5... | collective-permute-start | bytes 3145736 | tf_op jit(solution)/shard_map/ppermute | solution.py:68
  440.6 8.2 collective-permute-start.33
  448.9 13.4 %collective-permute-start.34 = (f32[64,512]{0,1:T(8,128)S(1)}, f32[64,512]{0,1:T(8,128)S(1)}, u32[]{:S(2)}, u32[]{:S(2)}) collective-permute-start(f32[64,512]{0,1:T(8,128)S(1)} %add.181), channel_id=1, source_target_pairs={{0,16},{4,20},{8,24},{12,28},{16,0},{20,4},{24,8},{28,12},{1,17},{... | collective-permute-start | bytes 393224 | tf_op jit(solution)/shard_map/ppermute | solution.py:81
  462.4 8.3 collective-permute-start.35
  470.9 9.2 collective-permute-start.36
  472.5 79.4 %collective-permute-start.26 = (f32[128,2048]{1,0:T(8,128)}, f32[128,2048]{1,0:T(8,128)}, u32[]{:S(2)}, u32[]{:S(2)}) collective-permute-start(f32[128,2048]{1,0:T(8,128)} %get-tuple-element.98), channel_id=1, source_target_pairs={{0,0},{4,4},{8,1},{12,5},{16,2},{20,6},{24,3},{28,7},{1,8},{5,12},... | collective-permute-start | bytes 3145736 | tf_op jit(solution)/shard_map/ppermute | solution.py:60
  474.4 92.4 %collective-permute-start.24 = (f32[128,2048]{1,0:T(8,128)}, f32[128,2048]{1,0:T(8,128)}, u32[]{:S(2)}, u32[]{:S(2)}) collective-permute-start(f32[128,2048]{1,0:T(8,128)} %get-tuple-element.97), channel_id=1, source_target_pairs={{0,0},{4,4},{8,1},{12,5},{16,2},{20,6},{24,3},{28,7},{1,8},{5,12},... | collective-permute-start | bytes 3145736 | tf_op jit(solution)/shard_map/ppermute | solution.py:60
  551.9 34.5 %collective-permute-start.27 = (f32[128,2048]{1,0:T(8,128)}, f32[128,2048]{1,0:T(8,128)}, u32[]{:S(2)}, u32[]{:S(2)}) collective-permute-start(f32[128,2048]{1,0:T(8,128)} %collective-permute-done.26), channel_id=1, source_target_pairs={{0,4},{4,0},{8,12},{12,8},{16,20},{20,16},{24,28},{28,24},{1,5},{5... | collective-permute-start | bytes 3145736 | tf_op jit(solution)/shard_map/ppermute | solution.py:68
  566.8 33.8 %collective-permute-start.25 = (f32[128,2048]{1,0:T(8,128)}, f32[128,2048]{1,0:T(8,128)}, u32[]{:S(2)}, u32[]{:S(2)}) collective-permute-start(f32[128,2048]{1,0:T(8,128)} %collective-permute-done.24), channel_id=1, source_target_pairs={{0,4},{4,0},{8,12},{12,8},{16,20},{20,16},{24,28},{28,24},{1,5},{5... | collective-permute-start | bytes 3145736 | tf_op jit(solution)/shard_map/ppermute | solution.py:68
  652.9 35.1 %collective-permute-start.41 = (f32[128,2304]{1,0:T(8,128)S(1)}, f32[128,2304]{1,0:T(8,128)}, u32[]{:S(2)}, u32[]{:S(2)}) collective-permute-start(f32[128,2304]{1,0:T(8,128)S(1)} %broadcast_select_fusion.1), channel_id=1, source_target_pairs={{0,1},{1,0},{2,3},{3,2},{4,5},{5,4},{6,7},{7,6},{8,9},{9,8},{10,11... | collective-permute-start | bytes 3538952 | tf_op jit(solution)/shard_map/ppermute | solution.py:81
  691.0 29.0 %collective-permute-start.42 = (f32[64,2304]{1,0:T(8,128)}, f32[64,2304]{1,0:T(8,128)}, u32[]{:S(2)}, u32[]{:S(2)}) collective-permute-start(f32[64,2304]{1,0:T(8,128)} %slice_select_fusion.6), channel_id=1, source_target_pairs={{0,2},{1,3},{2,0},{3,1},{4,6},{5,7},{6,4},{7,5},{8,10},{9,11},{10,... | collective-permute-start | bytes 1769480 | tf_op jit(solution)/shard_map/ppermute | solution.py:81
  721.2 4.3 collective-permute-start.45
  725.6 4.3 collective-permute-start.46
  726.8 14.9 %collective-permute-start.43 = (f32[64,2048]{1,0:T(8,128)S(1)}, f32[64,2048]{1,0:T(8,128)S(1)}, u32[]{:S(2)}, u32[]{:S(2)}) collective-permute-start(f32[64,2048]{1,0:T(8,128)S(1)} %slice.354), channel_id=1, source_target_pairs={{0,2},{1,3},{2,0},{3,1},{4,6},{5,7},{6,4},{7,5},{8,10},{9,11},{10,... | collective-permute-start | bytes 1572872 | tf_op jit(solution)/shard_map/ppermute | solution.py:81
  729.9 5.9 collective-permute-start.47
  735.9 5.7 collective-permute-start.48
  748.2 75.0 %collective-permute-start.52 = (f32[128,2048]{1,0:T(8,128)S(1)}, f32[128,2048]{1,0:T(8,128)}, u32[]{:S(2)}, u32[]{:S(2)}) collective-permute-start(f32[128,2048]{1,0:T(8,128)S(1)} %get-tuple-element.86), channel_id=1, source_target_pairs={{0,0},{4,4},{8,1},{12,5},{16,2},{20,6},{24,3},{28,7},{1,8},{5,12},... | collective-permute-start | bytes 3145736 | tf_op jit(solution)/shard_map/ppermute | solution.py:60
  752.5 92.9 %collective-permute-start.50 = (f32[128,2048]{1,0:T(8,128)S(1)}, f32[128,2048]{1,0:T(8,128)}, u32[]{:S(2)}, u32[]{:S(2)}) collective-permute-start(f32[128,2048]{1,0:T(8,128)S(1)} %get-tuple-element.85), channel_id=1, source_target_pairs={{0,0},{4,4},{8,1},{12,5},{16,2},{20,6},{24,3},{28,7},{1,8},{5,12},... | collective-permute-start | bytes 3145736 | tf_op jit(solution)/shard_map/ppermute | solution.py:60
  823.2 71.0 %collective-permute-start.53 = (f32[128,2048]{1,0:T(8,128)}, f32[128,2048]{1,0:T(8,128)}, u32[]{:S(2)}, u32[]{:S(2)}) collective-permute-start(f32[128,2048]{1,0:T(8,128)} %collective-permute-done.52), channel_id=1, source_target_pairs={{0,4},{4,0},{8,12},{12,8},{16,20},{20,16},{24,28},{28,24},{1,5},{5... | collective-permute-start | bytes 3145736 | tf_op jit(solution)/shard_map/ppermute | solution.py:68
  845.4 51.5 %collective-permute-start.51 = (f32[128,2048]{1,0:T(8,128)}, f32[128,2048]{1,0:T(8,128)}, u32[]{:S(2)}, u32[]{:S(2)}) collective-permute-start(f32[128,2048]{1,0:T(8,128)} %collective-permute-done.50), channel_id=1, source_target_pairs={{0,4},{4,0},{8,12},{12,8},{16,20},{20,16},{24,28},{28,24},{1,5},{5... | collective-permute-start | bytes 3145736 | tf_op jit(solution)/shard_map/ppermute | solution.py:68
  (74 other events, 1196.3 us)
